TPU v7x, 32 devices: a whole 2x2x4 slice. The times are simulated.
32 devices in a mesh: dp: 16 (over z, x, core), tensor: 2 (over y).
Axes of the slice: x: 2, y: 2, z: 4, core: 2. Of those that a mesh axis runs over, the one named last changes fastest.
Arguments:
- tokens: bfloat16 [1024, 16, 1024], P('tensor', 'dp'), may hold values from -6 to 6
- cond: bfloat16 [16, 1024], P('dp'), may hold values from -6 to 6
- qkv_weight: bfloat16 [1024, 3072], P('dp', 'tensor'), may hold values from -0.1875 to 0.1875
- out_weight: bfloat16 [1024, 1024], P('dp', 'tensor'), may hold values from -1.5 to 1.5
- up_weight: bfloat16 [1024, 4096], P('dp', 'tensor'), may hold values from -0.1875 to 0.1875
- down_weight: bfloat16 [1024, 4096], P('dp', 'tensor'), may hold values from -0.09375 to 0.09375
- ada_weight: bfloat16 [1024, 6144], P('dp'), may hold values from -0.1875 to 0.1875
- ada_bias: bfloat16 [6144], P('dp'), may hold values from -3 to 3
- cotangent: bfloat16 [1024, 16, 1024], P('tensor', 'dp'), may hold values from -6 to 6
Outputs:
- mixed: float32 [1024, 16, 1024], P('tensor', 'dp')
- grad_tokens: float32 [1024, 16, 1024], P('tensor', 'dp')
- grad_cond: float32 [16, 1024], P('dp')
- grad_qkv: float32 [1024, 3072], P('dp', 'tensor')
- grad_out: float32 [1024, 1024], P('dp', 'tensor')
- grad_up: float32 [1024, 4096], P('dp', 'tensor')
- grad_down: float32 [1024, 4096], P('dp', 'tensor')
- grad_ada: float32 [1024, 6144], P('dp')
- grad_ada_bias: float32 [6144], P('dp')
All inputs are finite; a program needn't handle non-finite values.
Results may differ from a plain program's by a relative error of at most 0.02.
The roundings to bfloat16 on the way count: a program that leaves them out, or rounds other values in their place, can miss the bound.
Values may be sent and summed in bfloat16 or wider, within the bound.
A program may use at most 192 MiB of HBM per device.

v0:
```python
import jax
import jax.numpy as jnp
from jax import lax
from jax.sharding import PartitionSpec as P

HEAD_DIM = 64


epsilon = 1e-06


def layer_norm(inputs):
    centred = inputs - jnp.mean(inputs, axis=-1, keepdims=True)
    return centred * lax.rsqrt(jnp.mean(centred * centred, axis=-1, keepdims=True) + epsilon)


def modulate(inputs, shift_vec, scale_vec):
    return layer_norm(inputs) * (1.0 + scale_vec) + shift_vec


def gelu_tanh(inputs):
    return jax.nn.gelu(inputs, approximate=True)


def gather_rows(local_part):
    return lax.all_gather(local_part, "tensor", axis=0, tiled=True)


def gather_grads(local_part):
    return lax.all_gather(local_part, "tensor", axis=0, tiled=True)


def scatter_rows(left_side, weight, local_rows):

    def term(first, length):
        return jnp.einsum("sle,fe->slf", left_side, weight, preferred_element_type=jnp.float32)

    return lax.psum_scatter(
        term(jnp.int32(0), lax.axis_size("tensor") * local_rows).astype(jnp.bfloat16),
        "tensor",
        scatter_dimension=0,
        tiled=True,
    ).astype(jnp.float32)


def scatter_grads(left_side, weight, local_rows):

    def term(first, length):
        return jnp.einsum("sle,fe->slf", left_side, weight, preferred_element_type=jnp.float32)

    return lax.psum_scatter(
        term(jnp.int32(0), lax.axis_size("tensor") * local_rows).astype(jnp.bfloat16),
        "tensor",
        scatter_dimension=0,
        tiled=True,
    ).astype(jnp.float32)


def split_heads(query_key_value):
    seq_len, latents, features = query_key_value.shape
    head_count = features // (3 * HEAD_DIM)
    divided = query_key_value.reshape(seq_len, latents, head_count, 3, HEAD_DIM).transpose(
        3, 1, 2, 0, 4
    )
    return (divided[0], divided[1], divided[2])


def attention_forward(queries, key_heads, value_heads, score_scale):
    latents, head_count, seq_len, head_width = queries.shape
    block_rows = min(512, seq_len)
    num_blocks = seq_len // block_rows

    def per_latent(inputs):
        query_lat, key_lat, value_lat = inputs

        def per_block(query_block):
            scores = (
                jnp.einsum("hqe,hke->hqk", query_block, key_lat, preferred_element_type=jnp.float32)
                * score_scale
            )
            row_max = jnp.max(scores, axis=-1, keepdims=True)
            shifted = jnp.exp(scores - row_max)
            denom_sum = jnp.sum(shifted, axis=-1, keepdims=True)
            weights = (shifted / denom_sum).astype(jnp.bfloat16)
            result = jnp.einsum(
                "hqk,hke->hqe", weights, value_lat, preferred_element_type=jnp.float32
            )
            return (result, (row_max + jnp.log(denom_sum))[:, :, 0])

        query_blocks = query_lat.reshape(head_count, num_blocks, block_rows, head_width).transpose(
            1, 0, 2, 3
        )
        results, log_parts = lax.map(per_block, query_blocks)
        results = results.transpose(1, 0, 2, 3).reshape(head_count, seq_len, head_width)
        log_parts = log_parts.transpose(1, 0, 2).reshape(head_count, seq_len)
        return (results, log_parts)

    results, log_total = lax.map(per_latent, (queries, key_heads, value_heads))
    attended = (
        results.transpose(2, 0, 1, 3)
        .reshape(seq_len, latents, head_count * head_width)
        .astype(jnp.bfloat16)
    )
    return (attended, log_total)


def attention_backward(queries, key_heads, value_heads, log_total, grad_heads, score_scale):
    latents, head_count, seq_len, head_width = queries.shape
    block_rows = min(512, seq_len)
    num_blocks = seq_len // block_rows

    def per_latent(inputs):
        query_lat, key_lat, value_lat, log_lat, grad_lat = inputs
        query_blocks = query_lat.reshape(head_count, num_blocks, block_rows, head_width).transpose(
            1, 0, 2, 3
        )
        grad_blocks = grad_lat.reshape(head_count, num_blocks, block_rows, head_width).transpose(
            1, 0, 2, 3
        )
        log_blocks = log_lat.reshape(head_count, num_blocks, block_rows).transpose(1, 0, 2)

        def advance(totals, pieces):
            grad_keys, grad_values = totals
            query_block, grad_block, log_block = pieces
            scores = (
                jnp.einsum("hqe,hke->hqk", query_block, key_lat, preferred_element_type=jnp.float32)
                * score_scale
            )
            probs = jnp.exp(scores - log_block[:, :, None])
            grad_probs = jnp.einsum(
                "hqe,hke->hqk", grad_block, value_lat, preferred_element_type=jnp.float32
            )
            delta = jnp.sum(grad_probs * probs, axis=-1, keepdims=True)
            grad_scores = (probs * (grad_probs - delta)).astype(jnp.bfloat16)
            grad_query = (
                jnp.einsum("hqk,hke->hqe", grad_scores, key_lat, preferred_element_type=jnp.float32)
                * score_scale
            )
            grad_keys = (
                grad_keys
                + jnp.einsum(
                    "hqk,hqe->hke", grad_scores, query_block, preferred_element_type=jnp.float32
                )
                * score_scale
            )
            grad_values = grad_values + jnp.einsum(
                "hqk,hqe->hke",
                probs.astype(jnp.bfloat16),
                grad_block,
                preferred_element_type=jnp.float32,
            )
            return ((grad_keys, grad_values), grad_query)

        zeros_init = jnp.zeros((head_count, seq_len, head_width), jnp.float32)
        (grad_keys, grad_values), grad_query = lax.scan(
            advance, (zeros_init, zeros_init), (query_blocks, grad_blocks, log_blocks)
        )
        grad_query = grad_query.transpose(1, 0, 2, 3).reshape(head_count, seq_len, head_width)
        return jnp.stack([grad_query, grad_keys, grad_values], 0)

    gradients = lax.map(per_latent, (queries, key_heads, value_heads, log_total, grad_heads))
    seq_first = gradients.transpose(3, 0, 2, 1, 4)
    return seq_first.reshape(seq_len, latents, head_count * 3 * head_width).astype(jnp.bfloat16)


def body(
    tokens, cond, qkv_weight, out_weight, up_weight, down_weight, ada_weight, ada_bias, cotangent
):
    local_rows = tokens.shape[0]
    latents = tokens.shape[1]
    score_scale = HEAD_DIM ** (-0.5)
    cond_value = cond.astype(jnp.float32)
    cond_act = jax.nn.silu(cond_value).astype(jnp.bfloat16)
    query_key_value_weight, expand_weight, w_out, w_down, full_bias, w_ada = (
        lax.all_gather(qkv_weight, "dp", axis=0, tiled=True),
        lax.all_gather(up_weight, "dp", axis=0, tiled=True),
        lax.all_gather(out_weight, "dp", axis=0, tiled=True),
        lax.all_gather(down_weight, "dp", axis=0, tiled=True),
        lax.all_gather(ada_bias, "dp", axis=0, tiled=True),
        lax.all_gather(ada_weight, "dp", axis=0, tiled=True),
    )
    modulation = jnp.dot(cond_act, w_ada, preferred_element_type=jnp.float32) + full_bias.astype(
        jnp.float32
    )
    shift1, scale1, gate1, shift2, scale2, gate2 = jnp.split(modulation, 6, axis=-1)
    residual = tokens.astype(jnp.float32)
    normed1 = modulate(residual, shift1, scale1).astype(jnp.bfloat16)
    complete_normed_first = gather_rows(normed1)
    query_key_value = jnp.einsum(
        "phg,gw->phw",
        complete_normed_first,
        query_key_value_weight,
        preferred_element_type=jnp.float32,
    ).astype(jnp.bfloat16)
    queries, key_heads, value_heads = split_heads(query_key_value)
    attended, log_total = attention_forward(queries, key_heads, value_heads, score_scale)
    branch = scatter_rows(attended, w_out, local_rows)
    middle = residual + gate1 * branch
    normed2 = modulate(middle, shift2, scale2).astype(jnp.bfloat16)
    complete_normed_second = gather_rows(normed2)
    hidden_activation = jnp.einsum(
        "phg,gw->phw", complete_normed_second, expand_weight, preferred_element_type=jnp.float32
    )
    activation = gelu_tanh(hidden_activation).astype(jnp.bfloat16)
    mlp_out = scatter_rows(activation, w_down, local_rows)
    mixed = middle + gate2 * mlp_out
    grad_output = cotangent.astype(jnp.float32)
    grad_gate2 = jnp.sum(grad_output * mlp_out, axis=0)
    grad_mlp = (grad_output * gate2).astype(jnp.bfloat16)
    full_grad_mlp = gather_grads(grad_mlp)
    grad_down = jnp.einsum(
        "slf,sle->fe", full_grad_mlp, activation, preferred_element_type=jnp.float32
    )
    grad_act = jnp.einsum("slf,fe->sle", full_grad_mlp, w_down, preferred_element_type=jnp.float32)
    gelu_pull = jax.vjp(gelu_tanh, hidden_activation)[1]
    hidden_gradient = gelu_pull(grad_act)[0].astype(jnp.bfloat16)
    grad_up = jnp.einsum(
        "knv,knj->vj", complete_normed_second, hidden_gradient, preferred_element_type=jnp.float32
    )
    grad_normed2 = scatter_grads(hidden_gradient, expand_weight, local_rows)
    mod_pull2 = jax.vjp(modulate, middle, shift2, scale2)[1]
    grad_middle, grad_shift2, grad_scale2 = mod_pull2(grad_normed2)
    grad_middle = grad_middle + grad_output
    grad_gate1 = jnp.sum(grad_middle * branch, axis=0)
    grad_branch = (grad_middle * gate1).astype(jnp.bfloat16)
    full_grad_branch = gather_grads(grad_branch)
    grad_out = jnp.einsum(
        "slf,sle->fe", full_grad_branch, attended, preferred_element_type=jnp.float32
    )
    grad_attended = jnp.einsum(
        "slf,fe->sle", full_grad_branch, w_out, preferred_element_type=jnp.float32
    ).astype(jnp.bfloat16)
    seq_len = grad_attended.shape[0]
    head_count = queries.shape[1]
    grad_heads = grad_attended.reshape(seq_len, latents, head_count, HEAD_DIM).transpose(1, 2, 0, 3)
    query_key_value_gradient_rows = attention_backward(
        queries, key_heads, value_heads, log_total, grad_heads, score_scale
    )
    grad_qkv = jnp.einsum(
        "knv,knj->vj",
        complete_normed_first,
        query_key_value_gradient_rows,
        preferred_element_type=jnp.float32,
    )
    grad_normed1 = scatter_grads(query_key_value_gradient_rows, query_key_value_weight, local_rows)
    mod_pull1 = jax.vjp(modulate, residual, shift1, scale1)[1]
    grad_residual, grad_shift1, grad_scale1 = mod_pull1(grad_normed1)
    grad_tokens = grad_residual + grad_middle
    mod_part = jnp.concatenate(
        [grad_shift1, grad_scale1, grad_gate1, grad_shift2, grad_scale2, grad_gate2], axis=-1
    )
    grad_mod = lax.psum(mod_part.astype(jnp.bfloat16), "tensor")
    grad_bias = jnp.sum(grad_mod.astype(jnp.float32), axis=0)
    grad_cond_act = jnp.einsum("lk,dk->ld", grad_mod, w_ada, preferred_element_type=jnp.float32)
    grad_ada = lax.psum_scatter(
        jnp.einsum("ld,lk->dk", cond_act, grad_mod, preferred_element_type=jnp.float32).astype(
            jnp.bfloat16
        ),
        "dp",
        scatter_dimension=0,
        tiled=True,
    ).astype(jnp.float32)
    sigmoid_c = jax.nn.sigmoid(cond_value)
    grad_cond = grad_cond_act * sigmoid_c * (1.0 + cond_value * (1.0 - sigmoid_c))
    grad_qkv, grad_up, grad_out, grad_down, grad_bias = (
        lax.psum_scatter(
            grad_qkv.astype(jnp.bfloat16), "dp", scatter_dimension=0, tiled=True
        ).astype(jnp.float32),
        lax.psum_scatter(
            grad_up.astype(jnp.bfloat16), "dp", scatter_dimension=0, tiled=True
        ).astype(jnp.float32),
        lax.psum_scatter(
            grad_out.astype(jnp.bfloat16), "dp", scatter_dimension=0, tiled=True
        ).astype(jnp.float32),
        lax.psum_scatter(
            grad_down.astype(jnp.bfloat16), "dp", scatter_dimension=0, tiled=True
        ).astype(jnp.float32),
        lax.psum_scatter(
            grad_bias.astype(jnp.bfloat16), "dp", scatter_dimension=0, tiled=True
        ).astype(jnp.float32),
    )
    return (
        mixed,
        grad_tokens,
        grad_cond,
        grad_qkv,
        grad_out,
        grad_up,
        grad_down,
        grad_ada,
        grad_bias,
    )


def solution(mesh):
    return jax.shard_map(
        body,
        mesh=mesh,
        in_specs=(
            P("tensor", "dp", None),
            P("dp", None),
            P("dp", "tensor"),
            P("dp", "tensor"),
            P("dp", "tensor"),
            P("dp", "tensor"),
            P("dp", None),
            P("dp"),
            P("tensor", "dp", None),
        ),
        out_specs=(
            P("tensor", "dp", None),
            P("tensor", "dp", None),
            P("dp", None),
            P("dp", "tensor"),
            P("dp", "tensor"),
            P("dp", "tensor"),
            P("dp", "tensor"),
            P("dp", None),
            P("dp"),
        ),
        check_vma=False,
    )
```

profile of v0, /device:TPU:0, one launch (start us, length us, event | category | flops | bytes accessed | tf_op | source)
XLA Modules:
  0.0 1135.0 jit_solution(16626235435518697479)
XLA Ops:
  9.4 23.5 %all-gather = bf16[16,1,384]{2,1,0:T(2,128)(2,1)S(1)} all-gather(bf16[1,1,384]{2,1,0:T(2,128)(2,1)S(1)} %reshape.442), channel_id=1, replica_groups=mesh['dp'=16,'tensor'=2] {'dp'}, dimensions={0}, use_global_device_ids=true | all-gather | bytes 13056 | tf_op jit(solution)/shard_map/all_gather | solution.py:179
  35.4 78.4 %all-gather.11.cloned.1.call-done = bf16[1024,6144]{1,0:T(8,128)(2,1)} async-done(((bf16[64,6144]{1,0:T(8,128)(2,1)}), bf16[1024,6144]{1,0:T(8,128)(2,1)}) %all-gather.11.cloned.1.call-update) | async-done | bytes 12582928 | tf_op jit(solution)/shard_map/all_gather | solution.py:180
  113.8 6.3 fusion.84
  123.6 35.9 %all-gather.15.cloned.1.call-done = bf16[1024,1536]{1,0:T(8,128)(2,1)} async-done(((bf16[64,1536]{1,0:T(8,128)(2,1)}), bf16[1024,1536]{1,0:T(8,128)(2,1)}) %all-gather.15.cloned.1.call-update) | async-done | bytes 3145744 | tf_op jit(solution)/shard_map/all_gather | solution.py:175
  159.5 34.1 %all-gather.13.cloned.1.call-done = bf16[1024,1,1024]{2,0,1:T(8,128)(2,1)} async-done(((bf16[512,1,1024]{2,0,1:T(8,128)(2,1)}), bf16[1024,1,1024]{2,0,1:T(8,128)(2,1)}) %all-gather.13.cloned.1.call-update) | async-done | bytes 2097168 | tf_op jit(solution)/shard_map/all_gather | solution.py:26
  193.6 5.9 convolution_convert_fusion.1
  199.5 2.9 copy.30
  202.4 3.2 slice_bitcast_fusion
  209.7 22.6 %while.45 = (s32[]{:T(128)}, bf16[2,8,512,64]{2,3,1,0:T(8,128)(2,1)}, f32[2,8,512]{2,1,0:T(8,128)S(1)}, bf16[2,8,512,64]{2,3,1,0:T(8,128)(2,1)S(1)}, bf16[8,1024...) while((s32[]{:T(128)}, bf16[2,8,512,64]{2,3,1,0:T(8,128)(2,1)}, ...), condition=%wide.region_5.6_spmd, body=%wide.region_2.5_spmd.sunk | while | flops 1111486464 | bytes 66715828 | solution.py:93
  209.7 2.5 multiply_reduce_fusion.5
  212.2 3.4 fusion.132
  215.6 4.3 fusion.133
  221.0 2.5 multiply_reduce_fusion.5
  223.5 3.4 fusion.132
  226.9 4.3 fusion.133
  232.3 3.7 copy.32
  235.9 2.6 convert_element_type.183
  238.5 4.2 convert_bitcast_fusion.3
  243.5 31.2 %reduce-scatter.10.cloned.1.call-done = bf16[512,1,1024]{2,0,1:T(8,128)(2,1)} async-done(((bf16[1024,1,1024]{2,0,1:T(8,128)(2,1)}), bf16[512,1,1024]{2,0,1:T(8,128)(2,1)}) %reduce-scatter.10.cloned.1.call-update) | async-done | bytes 1048592 | tf_op jit(solution)/shard_map/reduce_scatter | solution.py:38
  279.5 2.4 fusion.58
  282.0 45.5 %all-gather.21.cloned.1.call-done = bf16[1024,2048]{1,0:T(8,128)(2,1)} async-done(((bf16[64,2048]{1,0:T(8,128)(2,1)}), bf16[1024,2048]{1,0:T(8,128)(2,1)}) %all-gather.21.cloned.1.call-update) | async-done | bytes 4194320 | tf_op jit(solution)/shard_map/all_gather | solution.py:176
  327.5 33.8 %all-gather.19.cloned.1.call-done = bf16[1024,1,1024]{2,0,1:T(8,128)(2,1)} async-done(((bf16[512,1,1024]{2,0,1:T(8,128)(2,1)}), bf16[1024,1,1024]{2,0,1:T(8,128)(2,1)}) %all-gather.19.cloned.1.call-update) | async-done | bytes 2097168 | tf_op jit(solution)/shard_map/all_gather | solution.py:26
  361.3 10.7 fusion.70
  372.0 42.5 %all-gather.23.cloned.1.call-done = bf16[1024,2048]{1,0:T(8,128)(2,1)} async-done(((bf16[64,2048]{1,0:T(8,128)(2,1)}), bf16[1024,2048]{1,0:T(8,128)(2,1)}) %all-gather.23.cloned.1.call-update) | async-done | bytes 4194320 | tf_op jit(solution)/shard_map/all_gather | solution.py:178
  414.5 33.9 %all-gather.25.cloned.1.call-done = bf16[1024,1,1024]{2,0,1:T(8,128)(2,1)} async-done(((bf16[512,1,1024]{2,0,1:T(8,128)(2,1)}), bf16[1024,1,1024]{2,0,1:T(8,128)(2,1)}) %all-gather.25.cloned.1.call-update) | async-done | bytes 2097168 | tf_op jit(solution)/shard_map/all_gather | solution.py:30
  448.3 12.5 %fusion.39 = bf16[1024,2048]{1,0:T(8,128)(2,1)S(1)} fusion(f32[1024,2048]{1,0:T(8,128)} %fusion.70, bf16[1024,2048]{1,0:T(8,128)(2,1)} %all-gather.23.cloned.1.call-done, bf16[1024,1,1024]{2,0,1:T(8,128)(2,1)} %all-gather.25.cloned.1.call-done), kind=kOutput, calls=%fused_computation.50 | convolution fusion | flops 4336910336 | bytes 18874368 | tf_op jit(solution)/shard_map/slf,fe->sle/dot_general | solution.py:214
  462.8 5.7 convert_bitcast_fusion.1
  469.0 11.0 convert_bitcast_fusion.2
  480.1 20.4 %reduce-scatter.14.cloned.1.call-done = bf16[512,1,1024]{2,0,1:T(8,128)(2,1)} async-done(((bf16[1024,1,1024]{2,0,1:T(8,128)(2,1)}), bf16[512,1,1024]{2,0,1:T(8,128)(2,1)}) %reduce-scatter.14.cloned.1.call-update) | async-done | bytes 1048592 | tf_op jit(solution)/shard_map/reduce_scatter | solution.py:51
  502.9 3.3 fusion.54
  506.1 29.1 %reduce-scatter.12.cloned.1.call-done = bf16[512,1,1024]{2,0,1:T(8,128)(2,1)} async-done(((bf16[1024,1,1024]{2,0,1:T(8,128)(2,1)}), bf16[512,1,1024]{2,0,1:T(8,128)(2,1)}) %reduce-scatter.12.cloned.1.call-update) | async-done | bytes 1048592 | tf_op jit(solution)/shard_map/reduce_scatter | solution.py:38
  535.2 5.1 fusion.52
  543.0 33.2 %all-gather.27.cloned.1.call-done = bf16[1024,1,1024]{2,0,1:T(8,128)(2,1)} async-done(((bf16[512,1,1024]{2,0,1:T(8,128)(2,1)}), bf16[1024,1,1024]{2,0,1:T(8,128)(2,1)}) %all-gather.27.cloned.1.call-update) | async-done | bytes 2097168 | tf_op jit(solution)/shard_map/all_gather | solution.py:30
  576.2 3.1 fusion.76
  581.1 2.5 copy.33
  584.7 76.3 %while.46 = (s32[]{:T(128)}, f32[8,1024,64]{1,2,0:T(8,128)}, f32[8,1024,64]{1,2,0:T(8,128)}, bf16[2,8,512,64]{2,3,1,0:T(8,128)(2,1)}, bf16[2,8,512,64]{2,3,1,0:T...) while((s32[]{:T(128)}, f32[8,1024,64]{1,2,0:T(8,128)}, ...), condition=%wide.region_15.16_spmd.clone, body=%wide.region_13.15_spmd.clone.sunk | while | flops 2737565696 | bytes 178372816 | solution.py:155
  584.8 2.4 fusion.143
  587.1 4.5 select_add_fusion.5
  591.6 9.6 multiply_reduce_fusion.6
  601.2 10.4 multiply_convert_fusion.7
  611.6 7.0 fusion.144
  618.6 2.9 select_add_fusion.4
  623.9 5.7 select_add_fusion.5
  629.6 9.6 multiply_reduce_fusion.6
  639.2 10.4 multiply_convert_fusion.7
  649.6 7.0 fusion.144
  656.6 4.5 select_add_fusion.4
  664.4 2.8 fusion.40
  669.1 4.7 convert_bitcast_fusion
  673.9 10.7 convolution_convert_fusion.2
  685.0 9.3 convolution_convert_fusion.3
  694.4 4.2 fusion.79
  698.7 6.5 convolution_convert_fusion
  711.5 7.1 psum.7
  718.5 7.8 multiply_convert_fusion.1
  728.3 5.3 copy.36
  733.6 48.4 %reduce-scatter.24.cloned.1.call-done = bf16[64,2048]{1,0:T(8,128)(2,1)} async-done(((bf16[1024,2048]{1,0:T(8,128)(2,1)}), bf16[64,2048]{1,0:T(8,128)(2,1)}) %reduce-scatter.24.cloned.1.call-update) | async-done | bytes 262160 | tf_op jit(solution)/shard_map/reduce_scatter | solution.py:275
  783.8 74.1 %reduce-scatter.22.cloned.1.call-done = bf16[64,2048]{1,0:T(8,128)(2,1)} async-done(((bf16[1024,2048]{1,0:T(8,128)(2,1)}), bf16[64,2048]{1,0:T(8,128)(2,1)}) %reduce-scatter.22.cloned.1.call-update) | async-done | bytes 262160 | tf_op jit(solution)/shard_map/reduce_scatter | solution.py:269
  859.7 58.2 %reduce-scatter.20.cloned.1.call-done = bf16[64,512]{1,0:T(8,128)(2,1)} async-done(((bf16[1024,512]{1,0:T(8,128)(2,1)}), bf16[64,512]{1,0:T(8,128)(2,1)}) %reduce-scatter.20.cloned.1.call-update) | async-done | bytes 65552 | tf_op jit(solution)/shard_map/reduce_scatter | solution.py:272
  921.4 3.5 copy.37
  924.8 58.4 %all-reduce = bf16[6144]{0:T(1024)(128)(2,1)S(1)} all-reduce(bf16[6144]{0:T(1024)(128)(2,1)S(1)} %psum.7), channel_id=11, replica_groups=mesh['dp'=16,'tensor'=2] {'dp'}, use_global_device_ids=true, to_apply=%region_31.32.clone | all-reduce | flops 6144 | bytes 24576
  983.9 8.6 fusion.83
  994.2 131.4 %reduce-scatter.26.cloned.1.call-done = bf16[64,6144]{1,0:T(8,128)(2,1)} async-done(((bf16[1024,6144]{1,0:T(8,128)(2,1)}), bf16[64,6144]{1,0:T(8,128)(2,1)}) %reduce-scatter.26.cloned.1.call-update) | async-done | bytes 786448 | tf_op jit(solution)/shard_map/reduce_scatter | solution.py:255
  1125.6 2.4 convert_element_type.218
  (181 shorter events, 55.0 us)
Async XLA Ops:
  7.2 27.2 %copy-start.1 = (bf16[512,1,1024]{2,0,1:T(8,128)(2,1)S(1)}, bf16[512,1,1024]{2,0,1:T(8,128)(2,1)}, u32[]{:S(2)}) copy-start(bf16[512,1,1024]{2,0,1:T(8,128)(2,1)} %param.13) | copy-start | bytes 3145732
  7.2 106.7 %copy-start.22 = (bf16[1,1024]{1,0:T(2,128)(2,1)S(1)}, bf16[1,1024]{1,0:T(2,128)(2,1)}, u32[]{:S(2)}) copy-start(bf16[1,1024]{1,0:T(2,128)(2,1)} %param.14) | copy-start | bytes 6148
  7.2 106.6 %all-gather.11.cloned.1.call-start = ((), (), s32[]{:S(2)}) async-start(), calls=%async_computation.9 | async-start | bytes 13369344 | tf_op jit(solution)/shard_map/all_gather | solution.py:180
  7.9 151.6 %all-gather.15.cloned.1.call-start = ((), (), s32[]{:S(2)}) async-start(), calls=%async_computation.11 | async-start | bytes 3342336 | tf_op jit(solution)/shard_map/all_gather | solution.py:175
  8.7 184.9 %all-gather.13.cloned.1.call-start = ((), (), s32[]{:S(2)}) async-start(), calls=%async_computation.10 | async-start | bytes 3145728 | tf_op jit(solution)/shard_map/all_gather | solution.py:26
  34.4 86.4 %copy-start.20 = (f32[512]{0:T(512)}, f32[512]{0:T(512)S(1)}, u32[]{:S(2)}) copy-start(f32[512]{0:T(512)S(1)} %broadcast_multiply_fusion.1) | copy-start | bytes 6148
  34.8 0.6 copy-start.27
  35.4 85.4 %copy-start.25 = (f32[512]{0:T(512)}, f32[512]{0:T(512)S(1)}, u32[]{:S(2)}) copy-start(f32[512]{0:T(512)S(1)} %fusion.87) | copy-start | bytes 6148
  120.8 0.6 copy-start.18
  122.8 115.7 %all-gather.17.cloned.1.call-start = ((), (), s32[]{:S(2)}) async-start(), calls=%async_computation.12 | async-start | bytes 1114112 | tf_op jit(solution)/shard_map/all_gather | solution.py:177
  123.4 151.3 %reduce-scatter.10.cloned.1.call-start = ((), (), s32[]{:S(2)}) async-start(), calls=%async_computation.13 | async-start | bytes 3145728 | tf_op jit(solution)/shard_map/reduce_scatter | solution.py:38
  212.2 3.5 copy-start.7
  212.2 3.5 copy-start.14
  220.0 1.0 copy-start.15
  223.4 3.5 copy-start.7
  223.4 3.5 copy-start.14
  231.3 1.0 copy-start.15
  232.3 6.2 copy-start.4
  242.7 32.0 %copy-start.2 = (bf16[512,1,1024]{2,0,1:T(8,128)(2,1)S(1)}, bf16[512,1,1024]{2,0,1:T(8,128)(2,1)}, u32[]{:S(2)}) copy-start(bf16[512,1,1024]{2,0,1:T(8,128)(2,1)} %param.13) | copy-start | bytes 3145732
  242.7 32.0 %copy-start.16 = (f32[1,1024]{1,0:T(1,128)S(1)}, f32[1,1024]{1,0:T(1,128)}, u32[]{:S(2)}) copy-start(f32[1,1024]{1,0:T(1,128)} %get-tuple-element.260) | copy-start | bytes 12292
  242.7 84.8 %all-gather.21.cloned.1.call-start = ((), (), s32[]{:S(2)}) async-start(), calls=%async_computation.15 | async-start | bytes 4456448 | tf_op jit(solution)/shard_map/all_gather | solution.py:176
  243.3 118.1 %all-gather.19.cloned.1.call-start = ((), (), s32[]{:S(2)}) async-start(), calls=%async_computation.14 | async-start | bytes 3145728 | tf_op jit(solution)/shard_map/all_gather | solution.py:26
  274.7 1.8 copy-start.8
  274.7 2.4 copy-start.17
  274.7 2.4 copy-start.29
  277.1 2.4 copy-start.24
  278.7 135.8 %all-gather.23.cloned.1.call-start = ((), (), s32[]{:S(2)}) async-start(), calls=%async_computation.16 | async-start | bytes 4456448 | tf_op jit(solution)/shard_map/all_gather | solution.py:178
  279.4 168.9 %all-gather.25.cloned.1.call-start = ((), (), s32[]{:S(2)}) async-start(), calls=%async_computation.18 | async-start | bytes 3145728 | tf_op jit(solution)/shard_map/all_gather | solution.py:30
  282.0 218.5 %reduce-scatter.14.cloned.1.call-start = ((), (), s32[]{:S(2)}) async-start(), calls=%async_computation.19 | async-start | bytes 3145728 | tf_op jit(solution)/shard_map/reduce_scatter | solution.py:51
  448.3 14.5 %copy-start.33 = (bf16[1024,2048]{1,0:T(8,128)(2,1)S(1)}, bf16[1024,2048]{1,0:T(8,128)(2,1)}, u32[]{:S(2)}) copy-start(bf16[1024,2048]{1,0:T(8,128)(2,1)} %all-gather.21.cloned.1.call-done) | copy-start | bytes 12582916
  460.9 1.9 copy-start.36
  468.5 66.7 %reduce-scatter.12.cloned.1.call-start = ((), (), s32[]{:S(2)}) async-start(), calls=%async_computation.17 | async-start | bytes 3145728 | tf_op jit(solution)/shard_map/reduce_scatter | solution.py:38
  480.0 96.2 %all-gather.27.cloned.1.call-start = ((), (), s32[]{:S(2)}) async-start(), calls=%async_computation.20 | async-start | bytes 3145728 | tf_op jit(solution)/shard_map/all_gather | solution.py:30
  500.5 2.4 copy-start.12
  540.3 1.3 copy-start.9
  542.9 163.8 %reduce-scatter.16.cloned.1.call-start = ((), (), s32[]{:S(2)}) async-start(), calls=%async_computation.21 | async-start | bytes 3145728 | tf_op jit(solution)/shard_map/reduce_scatter | solution.py:51
  581.1 3.6 copy-start.5
  584.8 2.4 copy-start.6
  611.6 7.0 copy-start
  621.5 2.4 copy-start.6
  649.6 7.0 copy-start
  667.2 1.9 copy-start.34
  673.8 108.2 %reduce-scatter.24.cloned.1.call-start = ((), (), s32[]{:S(2)}) async-start(), calls=%async_computation.25 | async-start | bytes 4456448 | tf_op jit(solution)/shard_map/reduce_scatter | solution.py:275
  684.6 173.3 %reduce-scatter.22.cloned.1.call-start = ((), (), s32[]{:S(2)}) async-start(), calls=%async_computation.24 | async-start | bytes 4456448 | tf_op jit(solution)/shard_map/reduce_scatter | solution.py:269
  694.4 223.5 %reduce-scatter.20.cloned.1.call-start = ((), (), s32[]{:S(2)}) async-start(), calls=%async_computation.23 | async-start | bytes 1114112 | tf_op jit(solution)/shard_map/reduce_scatter | solution.py:272
  698.6 293.9 %reduce-scatter.18.cloned.1.call-start = ((), (), s32[]{:S(2)}) async-start(), calls=%async_computation.22 | async-start | bytes 3342336 | tf_op jit(solution)/shard_map/reduce_scatter | solution.py:266
  705.2 0.7 copy-start.23
  705.2 1.3 copy-start.13
  705.2 3.0 copy-start.3
  705.2 3.0 copy-start.19
  705.2 3.0 copy-start.21
  705.2 420.4 %reduce-scatter.26.cloned.1.call-start = ((), (), s32[]{:S(2)}) async-start(), calls=%async_computation.26 | async-start | bytes 13369344 | tf_op jit(solution)/shard_map/reduce_scatter | solution.py:255
  706.5 3.6 copy-start.28
  706.5 3.6 copy-start.26
  706.7 3.4 copy-start.11
  708.2 3.1 copy-start.32
  708.2 3.1 copy-start.30
  708.2 3.1 copy-start.31
  726.4 0.7 copy-start.35
  728.3 191.1 %copy-start.10 = (f32[512,1,1024]{2,0,1:T(8,128)S(1)}, f32[512,1,1024]{2,0,1:T(8,128)}, u32[]{:S(2)}) copy-start(f32[512,1,1024]{2,0,1:T(8,128)} %copy-done.9) | copy-start | bytes 6291460
Sparse Core Ops, SparseCore 0:
  10.3 103.4 all-gather.10
  116.1 43.3 all-gather.14
  161.6 31.9 all-gather.12
  195.6 37.9 all-gather.16
  242.8 31.8 reduce-scatter.9
  276.9 50.5 all-gather.20
  329.7 31.6 all-gather.18
  363.7 50.7 all-gather.22
  416.7 31.6 all-gather.24
  468.6 31.8 reduce-scatter.13
  503.3 31.8 reduce-scatter.11
  543.0 33.1 all-gather.26
  673.9 31.8 reduce-scatter.15
  709.5 72.4 reduce-scatter.23
  786.2 71.6 reduce-scatter.21
  861.4 56.4 reduce-scatter.19
  922.0 65.4 reduce-scatter.17
  991.9 133.6 reduce-scatter.25
where the time goes:
time: 1140 us
  waiting for transfers between devices  733 us (64%)
  matrix products  173 us (15%)
  blocking collectives  89 us (8%)
  other arithmetic  77.2 us (7%)
  local copies, waits for them, and re-layouts  45.2 us (4%)
  between operations  15.6 us (1%)
    reduce_scatter x1, waiting for transfers between devices, body(): lax.psum_scatter(jnp.einsum('ld,lk->dk', cond_act, grad_mod, preferred_el...  131 us
    all_gather x1, waiting for transfers between devices, body(): lax.all_gather(ada_weight, 'dp', axis=0, tiled=True)  78.4 us
    reduce_scatter x1, waiting for transfers between devices, body(): lax.psum_scatter(grad_up.astype(jnp.bfloat16), 'dp', scatter_dimension=0,...  74.1 us
    all_gather x2, waiting for transfers between devices, gather_rows(): return lax.all_gather(local_part, 'tensor', axis=0, tiled=True)  67.9 us
    all_gather x2, waiting for transfers between devices, gather_grads(): return lax.all_gather(local_part, 'tensor', axis=0, tiled=True)  67.1 us
    reduce_scatter x2, waiting for transfers between devices, scatter_rows(): lax.psum_scatter(term(jnp.int32(0), lax.axis_size('tensor') * local_rows)...  60.2 us
    unnamed x1, blocking collectives  58.4 us
    reduce_scatter x1, waiting for transfers between devices, body(): lax.psum_scatter(grad_out.astype(jnp.bfloat16), 'dp', scatter_dimension=0...  58.2 us
  transfers between devices with their start and end apart: 18, of which 15 were waited for; matrix products, arithmetic and copies ran while one was open for 14% of the time, Pallas kernels for 0%

commit v1 on v0

v1 whole, which is shorter than its diff:
```python
import jax
import jax.numpy as jnp
from jax import lax
from jax.sharding import PartitionSpec as P

HEAD_DIM = 64


epsilon = 1e-06


def layer_norm(inputs):
    centred = inputs - jnp.mean(inputs, axis=-1, keepdims=True)
    return centred * lax.rsqrt(jnp.mean(centred * centred, axis=-1, keepdims=True) + epsilon)


def modulate(inputs, shift_vec, scale_vec):
    return layer_norm(inputs) * (1.0 + scale_vec) + shift_vec


def gelu_tanh(inputs):
    return jax.nn.gelu(inputs, approximate=True)


def split_heads(query_key_value):
    latents, seq_len, features = query_key_value.shape
    head_count = features // (3 * HEAD_DIM)
    divided = query_key_value.reshape(latents, seq_len, head_count, 3, HEAD_DIM).transpose(
        3, 0, 2, 1, 4
    )
    return (divided[0], divided[1], divided[2])


def attention_forward(query_key_value, score_scale):
    queries, key_heads, value_heads = split_heads(query_key_value)
    latents, head_count, seq_len, head_width = queries.shape
    block_rows = min(512, seq_len)
    num_blocks = seq_len // block_rows

    def per_latent(inputs):
        query_lat, key_lat, value_lat = inputs

        def per_block(query_block):
            scores = (
                jnp.einsum("hqe,hke->hqk", query_block, key_lat, preferred_element_type=jnp.float32)
                * score_scale
            )
            row_max = jnp.max(scores, axis=-1, keepdims=True)
            shifted = jnp.exp(scores - row_max)
            denom_sum = jnp.sum(shifted, axis=-1, keepdims=True)
            weights = (shifted / denom_sum).astype(jnp.bfloat16)
            result = jnp.einsum(
                "hqk,hke->hqe", weights, value_lat, preferred_element_type=jnp.float32
            )
            return (result, (row_max + jnp.log(denom_sum))[:, :, 0])

        query_blocks = query_lat.reshape(head_count, num_blocks, block_rows, head_width).transpose(
            1, 0, 2, 3
        )
        results, log_parts = lax.map(per_block, query_blocks)
        results = results.transpose(1, 0, 2, 3).reshape(head_count, seq_len, head_width)
        log_parts = log_parts.transpose(1, 0, 2).reshape(head_count, seq_len)
        return (results, log_parts)

    results, log_total = lax.map(per_latent, (queries, key_heads, value_heads))
    attended = (
        results.transpose(0, 2, 1, 3)
        .reshape(latents, seq_len, head_count * head_width)
        .astype(jnp.bfloat16)
    )
    return (attended, log_total)


def attention_backward(query_key_value, attended, log_total, grad_attended, score_scale):
    queries, key_heads, value_heads = split_heads(query_key_value)
    latents, head_count, seq_len, head_width = queries.shape
    grad_heads = grad_attended.reshape(latents, seq_len, head_count, head_width).transpose(
        0, 2, 1, 3
    )
    block_rows = min(512, seq_len)
    num_blocks = seq_len // block_rows

    def per_latent(inputs):
        query_lat, key_lat, value_lat, log_lat, grad_lat = inputs
        query_blocks = query_lat.reshape(head_count, num_blocks, block_rows, head_width).transpose(
            1, 0, 2, 3
        )
        grad_blocks = grad_lat.reshape(head_count, num_blocks, block_rows, head_width).transpose(
            1, 0, 2, 3
        )
        log_blocks = log_lat.reshape(head_count, num_blocks, block_rows).transpose(1, 0, 2)

        def advance(totals, pieces):
            grad_keys, grad_values = totals
            query_block, grad_block, log_block = pieces
            scores = (
                jnp.einsum("hqe,hke->hqk", query_block, key_lat, preferred_element_type=jnp.float32)
                * score_scale
            )
            probs = jnp.exp(scores - log_block[:, :, None])
            grad_probs = jnp.einsum(
                "hqe,hke->hqk", grad_block, value_lat, preferred_element_type=jnp.float32
            )
            delta = jnp.sum(grad_probs * probs, axis=-1, keepdims=True)
            grad_scores = (probs * (grad_probs - delta)).astype(jnp.bfloat16)
            grad_query = (
                jnp.einsum("hqk,hke->hqe", grad_scores, key_lat, preferred_element_type=jnp.float32)
                * score_scale
            )
            grad_keys = (
                grad_keys
                + jnp.einsum(
                    "hqk,hqe->hke", grad_scores, query_block, preferred_element_type=jnp.float32
                )
                * score_scale
            )
            grad_values = grad_values + jnp.einsum(
                "hqk,hqe->hke",
                probs.astype(jnp.bfloat16),
                grad_block,
                preferred_element_type=jnp.float32,
            )
            return ((grad_keys, grad_values), grad_query)

        zeros_init = jnp.zeros((head_count, seq_len, head_width), jnp.float32)
        (grad_keys, grad_values), grad_query = lax.scan(
            advance, (zeros_init, zeros_init), (query_blocks, grad_blocks, log_blocks)
        )
        grad_query = grad_query.transpose(1, 0, 2, 3).reshape(head_count, seq_len, head_width)
        return jnp.stack([grad_query, grad_keys, grad_values], 0)

    gradients = lax.map(per_latent, (queries, key_heads, value_heads, log_total, grad_heads))
    seq_first = gradients.transpose(0, 3, 2, 1, 4)
    return seq_first.reshape(latents, seq_len, head_count * 3 * head_width).astype(jnp.bfloat16)


def dp_partner(value, bit):
    size = lax.axis_size("dp")
    return lax.ppermute(value, "dp", [(index, index ^ bit) for index in range(size)])


def gather_small(value):
    size, me, bit = lax.axis_size("dp"), lax.axis_index("dp"), 1
    while bit < size:
        other = dp_partner(value, bit)
        upper = (me & bit) != 0
        value = jnp.concatenate([jnp.where(upper, other, value), jnp.where(upper, value, other)], axis=0)
        bit *= 2
    return value


def scatter_small(value):
    me, bit = lax.axis_index("dp"), lax.axis_size("dp") // 2
    while bit >= 1:
        half = value.shape[0] // 2
        upper = (me & bit) != 0
        low_half, high_half = value[:half], value[half:]
        kept = jnp.where(upper, high_half, low_half)
        value = kept + dp_partner(jnp.where(upper, low_half, high_half), bit)
        bit //= 2
    return value


def swap(value):
    return lax.ppermute(value, "tensor", [(0, 1), (1, 0)])


def spread(own):
    if lax.axis_size("tensor") == 2:
        return [own, swap(own)]
    return [lax.all_gather(own, "tensor", axis=1, tiled=True)]


def joined(parts):
    return parts[0] if len(parts) == 1 else jnp.concatenate(parts, axis=1)


def collect(parts, weight):
    def term(part):
        return jnp.einsum("lse,fe->lsf", part, weight, preferred_element_type=jnp.float32).astype(
            jnp.bfloat16
        )

    if len(parts) == 2:
        arrived = swap(term(parts[1]))
        return term(parts[0]).astype(jnp.float32) + arrived.astype(jnp.float32)
    return lax.psum_scatter(term(parts[0]), "tensor", scatter_dimension=1, tiled=True).astype(
        jnp.float32
    )


def body(
    tokens, cond, qkv_weight, out_weight, up_weight, down_weight, ada_weight, ada_bias, cotangent
):
    me = lax.axis_index("dp")
    width = tokens.shape[2]
    score_scale = HEAD_DIM ** (-0.5)
    qkv_columns, up_columns = qkv_weight.shape[1], up_weight.shape[1]
    first_weights = lax.all_gather(
        jnp.concatenate([qkv_weight, out_weight], axis=1), "dp", axis=0, tiled=True
    )
    second_weights = lax.all_gather(
        jnp.concatenate([up_weight, down_weight], axis=1), "dp", axis=0, tiled=True
    )
    w_qkv, w_out = first_weights[:, :qkv_columns], first_weights[:, qkv_columns:]
    w_up, w_down = second_weights[:, :up_columns], second_weights[:, up_columns:]
    own_tokens = tokens.transpose(1, 0, 2)
    own_cotangent = cotangent.transpose(1, 0, 2)
    token_parts = spread(own_tokens)
    cotangent_parts = spread(own_cotangent)
    cond_value = cond.astype(jnp.float32)
    cond_act = jax.nn.silu(cond_value).astype(jnp.bfloat16)
    all_cond_act = gather_small(cond_act)
    ada_rows, ada_columns = ada_weight.shape
    bias_columns = ada_bias.shape[0]
    my_cond_act = lax.dynamic_slice_in_dim(all_cond_act, me * ada_rows, ada_rows, axis=1)
    mod_term = jnp.dot(my_cond_act, ada_weight, preferred_element_type=jnp.float32)
    placed_bias = lax.dynamic_update_slice_in_dim(
        jnp.zeros((ada_columns,), jnp.float32),
        ada_bias.astype(jnp.float32),
        me * bias_columns,
        axis=0,
    )
    modulation = scatter_small(mod_term + placed_bias[None, :])
    shift1, scale1, gate1, shift2, scale2, gate2 = jnp.split(modulation[:, None, :], 6, axis=-1)
    residual = own_tokens.astype(jnp.float32)
    full_normed1 = joined(
        [
            modulate(part.astype(jnp.float32), shift1, scale1).astype(jnp.bfloat16)
            for part in token_parts
        ]
    )
    query_key_value = jnp.einsum(
        "lsd,dw->lsw", full_normed1, w_qkv, preferred_element_type=jnp.float32
    ).astype(jnp.bfloat16)
    attended, log_total = attention_forward(query_key_value, score_scale)
    own_count = residual.shape[1]
    attended_parts = (
        [attended[:, :own_count], attended[:, own_count:]] if len(token_parts) == 2 else [attended]
    )
    branch = collect(attended_parts, w_out)
    middle = residual + gate1 * branch
    normed2 = modulate(middle, shift2, scale2).astype(jnp.bfloat16)
    normed2_parts = spread(normed2)
    inner_parts = [
        jnp.einsum("lsd,dw->lsw", part, w_up, preferred_element_type=jnp.float32)
        for part in normed2_parts
    ]
    activation_parts = [gelu_tanh(part).astype(jnp.bfloat16) for part in inner_parts]
    mlp_out = collect(activation_parts, w_down)
    mixed = middle + gate2 * mlp_out
    grad_output = own_cotangent.astype(jnp.float32)
    grad_gate2 = jnp.sum(grad_output * mlp_out, axis=1)
    grad_mlp_parts = [
        (part.astype(jnp.float32) * gate2).astype(jnp.bfloat16) for part in cotangent_parts
    ]
    grad_inner_parts = []
    for grad_part, inner_part in zip(grad_mlp_parts, inner_parts):
        grad_act = jnp.einsum("lsf,fe->lse", grad_part, w_down, preferred_element_type=jnp.float32)
        grad_inner_parts.append(
            jax.vjp(gelu_tanh, inner_part)[1](grad_act)[0].astype(jnp.bfloat16)
        )
    grad_normed2 = collect(grad_inner_parts, w_up)
    grad_down = jnp.einsum(
        "lsf,lse->fe",
        joined(grad_mlp_parts),
        joined(activation_parts),
        preferred_element_type=jnp.float32,
    )
    grad_up = jnp.einsum(
        "lsd,lse->de",
        joined(normed2_parts),
        joined(grad_inner_parts),
        preferred_element_type=jnp.float32,
    )
    second_grads = jnp.concatenate(
        [grad_up.astype(jnp.bfloat16), grad_down.astype(jnp.bfloat16)], axis=1
    )
    mod_pull2 = jax.vjp(modulate, middle, shift2, scale2)[1]
    grad_middle, grad_shift2, grad_scale2 = mod_pull2(grad_normed2)
    grad_middle = grad_middle + grad_output
    grad_gate1 = jnp.sum(grad_middle * branch, axis=1)
    grad_branch = (grad_middle * gate1).astype(jnp.bfloat16)
    full_grad_branch = joined(spread(grad_branch))
    full_grad_branch, second_grads = lax.optimization_barrier((full_grad_branch, second_grads))
    second_grads = lax.psum_scatter(second_grads, "dp", scatter_dimension=0, tiled=True)
    grad_attended = jnp.einsum(
        "lsf,fe->lse", full_grad_branch, w_out, preferred_element_type=jnp.float32
    ).astype(jnp.bfloat16)
    grad_out = jnp.einsum(
        "lsf,lse->fe", full_grad_branch, attended, preferred_element_type=jnp.float32
    ).astype(jnp.bfloat16)
    grad_query_key_value = attention_backward(
        query_key_value, attended, log_total, grad_attended, score_scale
    )
    grad_qkv = jnp.einsum(
        "lsd,lsw->dw", full_normed1, grad_query_key_value, preferred_element_type=jnp.float32
    ).astype(jnp.bfloat16)
    first_grads = lax.psum_scatter(
        jnp.concatenate([grad_qkv, grad_out], axis=1), "dp", scatter_dimension=0, tiled=True
    )
    grad_parts = (
        [grad_query_key_value[:, :own_count], grad_query_key_value[:, own_count:]]
        if len(token_parts) == 2
        else [grad_query_key_value]
    )
    grad_normed1 = collect(grad_parts, w_qkv)
    mod_pull1 = jax.vjp(modulate, residual, shift1, scale1)[1]
    grad_residual, grad_shift1, grad_scale1 = mod_pull1(grad_normed1)
    grad_tokens = grad_residual + grad_middle
    mod_part = jnp.concatenate(
        [
            grad_shift1[:, 0],
            grad_scale1[:, 0],
            grad_gate1,
            grad_shift2[:, 0],
            grad_scale2[:, 0],
            grad_gate2,
        ],
        axis=-1,
    )
    if lax.axis_size("tensor") == 2:
        mod_sum = mod_part + swap(mod_part)
    else:
        mod_sum = lax.psum(mod_part, "tensor")
    all_grad_mod = gather_small(mod_sum.astype(jnp.bfloat16))
    grad_bias = jnp.sum(
        lax.dynamic_slice_in_dim(all_grad_mod, me * bias_columns, bias_columns, axis=1).astype(
            jnp.float32
        ),
        axis=0,
    )
    grad_ada = jnp.einsum(
        "ld,lk->dk", my_cond_act, all_grad_mod, preferred_element_type=jnp.float32
    )
    cond_term = jnp.einsum(
        "lk,dk->ld", all_grad_mod, ada_weight, preferred_element_type=jnp.float32
    )
    grad_cond_act = scatter_small(
        lax.dynamic_update_slice_in_dim(
            jnp.zeros((cond_term.shape[0], width), jnp.float32), cond_term, me * ada_rows, axis=1
        )
    )
    sigmoid_c = jax.nn.sigmoid(cond_value)
    grad_cond = grad_cond_act * sigmoid_c * (1.0 + cond_value * (1.0 - sigmoid_c))
    return (
        mixed.transpose(1, 0, 2),
        grad_tokens.transpose(1, 0, 2),
        grad_cond,
        first_grads[:, :qkv_columns].astype(jnp.float32),
        first_grads[:, qkv_columns:].astype(jnp.float32),
        second_grads[:, :up_columns].astype(jnp.float32),
        second_grads[:, up_columns:].astype(jnp.float32),
        grad_ada,
        grad_bias,
    )


def solution(mesh):
    return jax.shard_map(
        body,
        mesh=mesh,
        in_specs=(
            P("tensor", "dp", None),
            P("dp", None),
            P("dp", "tensor"),
            P("dp", "tensor"),
            P("dp", "tensor"),
            P("dp", "tensor"),
            P("dp", None),
            P("dp"),
            P("tensor", "dp", None),
        ),
        out_specs=(
            P("tensor", "dp", None),
            P("tensor", "dp", None),
            P("dp", None),
            P("dp", "tensor"),
            P("dp", "tensor"),
            P("dp", "tensor"),
            P("dp", "tensor"),
            P("dp", None),
            P("dp"),
        ),
        check_vma=False,
    )
```

time: 1140 us -> 574 us (0.50)
  waiting for transfers between devices: 733 us -> 236 us
  blocking collectives: 89 us -> 0 us
  starting transfers between devices: 1.93 us -> 30.8 us
  matrix products: 173 us -> 160 us
    all_gather x9 -> x2, waiting for transfers between devices: 337 us -> 13.2 us  [the longest x1 13.2 us: body(): lax.all_gather(jnp.concatenate([qkv_weight, out_weight], axis=1), 'dp', a...]
    reduce_scatter x9 -> x2, waiting for transfers between devices: 393 us -> 77.3 us  [the longest x1 77.3 us: body(): lax.psum_scatter(second_grads, 'dp', scatter_dimension=0, tiled=True)]
    ppermute x0 -> x25, waiting for transfers between devices: none -> 145 us  [the longest x9 100 us: swap(): return lax.ppermute(value, 'tensor', [(0, 1), (1, 0)])]
    unnamed x1 -> x0, blocking collectives: 58.4 us -> none
    ppermute x0 -> x25, starting transfers between devices: none -> 30.7 us  [the longest x16 19.6 us: dp_partner(): lax.ppermute(value, 'dp', [(index, index ^ bit) for index in range(size)])]
    all_gather x1 -> x0, blocking collectives: 23.5 us -> none  [body(): lax.all_gather(ada_bias, 'dp', axis=0, tiled=True)]
    dot_general x14 -> x21, matrix products: 103 us -> 86.2 us  [the longest x8 32.8 us: term(): jnp.einsum('lse,fe->lsf', part, weight, preferred_element_type=jnp.float32)]
    concatenate x1 -> x11, other arithmetic: 0.07 us -> 16.2 us  [the longest x1 7.85 us: body(): jnp.concatenate([grad_up.astype(jnp.bfloat16), grad_down.astype(jnp.bfloa...]
  transfers between devices with their start and end apart: 18 -> 29, of which waited for: 15 -> 24; matrix products, arithmetic and copies ran while one was open for 14% -> 26% of each run, Pallas kernels for 0% -> 0%
where the time goes in v1:
time: 574 us; the launch traced here: 564 us
  waiting for transfers between devices  236 us (41%)
  matrix products  160 us (28%)
  other arithmetic  75.9 us (13%)
  local copies, waits for them, and re-layouts  46.5 us (8%)
  starting transfers between devices  30.8 us (5%)
  between operations  14.9 us (3%)
    ppermute x9, waiting for transfers between devices, swap(): return lax.ppermute(value, 'tensor', [(0, 1), (1, 0)])  100 us
    reduce_scatter x1, waiting for transfers between devices, body(): lax.psum_scatter(second_grads, 'dp', scatter_dimension=0, tiled=True)  77.3 us
    ppermute x16, waiting for transfers between devices, dp_partner(): lax.ppermute(value, 'dp', [(index, index ^ bit) for index in range(size)])  44.7 us
    dot_general x8, matrix products, term(): jnp.einsum('lse,fe->lsf', part, weight, preferred_element_type=jnp.float32)  32.8 us
    convert_element_type x2, other arithmetic, advance(): grad_scores = (probs * (grad_probs - delta)).astype(jnp.bfloat16)  20.8 us
    ppermute x16, starting transfers between devices, dp_partner(): lax.ppermute(value, 'dp', [(index, index ^ bit) for index in range(size)])  19.6 us
    dot_general x2, matrix products, advance(): jnp.einsum('hqe,hke->hqk', grad_block, value_lat, preferred_element_type=...  19.3 us
    unnamed x108, local copies, waits for them, and re-layouts  16.3 us
  transfers between devices with their start and end apart: 29, of which 24 were waited for; matrix products, arithmetic and copies ran while one was open for 26% of the time, Pallas kernels for 0%

profile of v1, /device:TPU:0, one launch (start us, length us, event | category | flops | bytes accessed | tf_op | source)
XLA Modules:
  0.0 563.6 jit_solution(7498847657154223613)
XLA Ops:
  11.7 2.9 collective-permute-start.1
  20.1 3.1 collective-permute-start.3
  26.4 3.1 collective-permute-start.4
  31.6 10.7 %collective-permute-done.4 = f32[8,6144]{1,0:T(8,128)S(1)} collective-permute-done((f32[8,6144]{1,0:T(8,128)}, f32[8,6144]{1,0:T(8,128)S(1)}, u32[]{:S(2)}, u32[]{:S(2)}) %collective-permute-start.4) | collective-permute-done | bytes 196640 | tf_op jit(solution)/shard_map/ppermute | solution.py:139
  42.5 4.6 collective-permute-done.5
  49.1 3.2 collective-permute-done.6
  57.2 13.2 %all-gather.3.cloned.1.call-done = bf16[1024,2048]{1,0:T(8,128)(2,1)} async-done(((bf16[64,2048]{1,0:T(8,128)(2,1)}), bf16[1024,2048]{1,0:T(8,128)(2,1)}) %all-gather.3.cloned.1.call-update) | async-done | bytes 4194320 | tf_op jit(solution)/shard_map/all_gather | solution.py:199
  70.4 7.6 %convolution_convert_fusion.1 = bf16[1024,1536]{1,0:T(8,128)(2,1)} fusion(bf16[1024,2048]{1,0:T(8,128)(2,1)} %all-gather.3.cloned.1.call-done, bf16[1,512,1024]{2,1,0:T(8,128)(2,1)} %get-tuple-element.272, bf16[1,512,1024]{2,1,0:T(8,128)(2,1)} %get-tuple-element.271), kind=kOutput, calls=%fused_computation.76 | convolution fusion | flops 3226992640 | bytes 8388608 | tf_op jit(solution)/shard_map/lsd,dw->lsw/dot_general | solution.py:233
  78.0 4.7 copy.23
  82.6 3.5 slice_bitcast_fusion.12
  92.3 24.7 %while.45 = (s32[]{:T(128)}, bf16[2,8,512,64]{2,3,1,0:T(8,128)(2,1)}, f32[2,8,512]{2,1,0:T(8,128)S(1)}, bf16[2,8,512,64]{2,3,1,0:T(8,128)(2,1)}, bf16[8,1024,64]...) while((s32[]{:T(128)}, bf16[2,8,512,64]{2,3,1,0:T(8,128)(2,1)}, ...), condition=%wide.region_7.8_spmd, body=%wide.region_4.7_spmd.sunk | while | flops 1111486464 | bytes 66715828 | solution.py:60
  92.3 3.5 multiply_reduce_fusion.8
  95.8 3.4 fusion.219
  99.3 4.3 fusion.220
  104.6 3.5 multiply_reduce_fusion.8
  108.2 3.4 fusion.219
  111.6 4.3 fusion.220
  117.0 3.3 copy.25
  120.2 3.0 convert_element_type.319
  127.5 24.0 %collective-permute-done.9 = bf16[1,512,1024]{2,1,0:T(8,128)(2,1)S(1)} collective-permute-done((bf16[1,512,1024]{2,1,0:T(8,128)(2,1)S(1)}, bf16[1,512,1024]{2,1,0:T(8,128)(2,1)S(1)}, u32[]{:S(2)}, u32[]{:S(2)}) %collective-permute-start.9) | collective-permute-done | bytes 1048608 | tf_op jit(solution)/shard_map/ppermute | solution.py:165
  151.5 4.0 fusion.187
  159.7 14.4 %collective-permute-done.12 = bf16[1,512,1024]{2,1,0:T(8,128)(2,1)} collective-permute-done((bf16[1,512,1024]{2,1,0:T(8,128)(2,1)}, bf16[1,512,1024]{2,1,0:T(8,128)(2,1)}, u32[]{:S(2)}, u32[]{:S(2)}) %collective-permute-start.12) | collective-permute-done | bytes 1048608 | tf_op jit(solution)/shard_map/ppermute | solution.py:165
  176.5 19.4 %collective-permute-done.10 = bf16[1,512,1024]{2,1,0:T(8,128)(2,1)} collective-permute-done((bf16[1,512,1024]{2,1,0:T(8,128)(2,1)}, bf16[1,512,1024]{2,1,0:T(8,128)(2,1)}, u32[]{:S(2)}, u32[]{:S(2)}) %collective-permute-start.10) | collective-permute-done | bytes 1048608 | tf_op jit(solution)/shard_map/ppermute | solution.py:165
  195.8 5.0 fusion.72
  202.9 4.6 fusion.46
  211.5 3.6 fusion.74
  215.1 4.9 fusion.39
  221.3 7.9 %fusion.54 = bf16[1024,2048]{1,0:T(8,128)(2,1)} fusion(bf16[1,512,2048]{2,1,0:T(8,128)(2,1)S(1)} %bitcast.290, bf16[1,512,2048]{2,1,0:T(8,128)(2,1)S(1)} %bitcast.289, bf16[1,512,1024]{2,1,0:T(8,128)(2,1)} %collective-permute-done.10, bf16[1,512,1024]{2,1,0:T(8,128)(2,1)} %add_convert_fusion), kind=kOutput, calls=%fused_computation.74 | convolution fusion | flops 4309647360 | bytes 10485760 | tf_op jit(solution)/shard_map/lsd,lse->de/dot_general | solution.py:270
  229.3 5.2 collective-permute-done.13
  234.5 3.5 multiply_reduce_fusion.2
  243.2 6.7 %fusion.53 = bf16[1024,2048]{1,0:T(8,128)(2,1)} fusion(bf16[1,512,2048]{2,1,0:T(8,128)(2,1)S(1)} %fusion.185, bf16[1,512,2048]{2,1,0:T(8,128)(2,1)S(1)} %fusion.184, bf16[1,512,1024]{2,1,0:T(8,128)(2,1)S(1)} %copy-done.26, bf16[1,512,1024]{2,1,0:T(8,128)(2,1)S(1)} %get-tuple-element.249), kind=kOutput, calls=%fused_computation.73 | convolution fusion | flops 4309647360 | bytes 10485760 | tf_op jit(solution)/shard_map/lsf,lse->fe/dot_general | solution.py:264
  249.9 7.8 %pad_maximum_fusion = bf16[1024,4096]{1,0:T(8,128)(2,1)} fusion(bf16[1024,2048]{1,0:T(8,128)(2,1)} %fusion.53, bf16[1024,2048]{1,0:T(8,128)(2,1)} %fusion.54), kind=kLoop, calls=%fused_computation.41 | loop fusion | flops 16777216 | bytes 16777216 | tf_op jit(solution)/shard_map/concatenate | solution.py:276
  257.8 7.9 %collective-permute-done.14 = bf16[1,512,1024]{2,1,0:T(8,128)(2,1)} collective-permute-done((bf16[1,512,1024]{2,1,0:T(8,128)(2,1)}, bf16[1,512,1024]{2,1,0:T(8,128)(2,1)}, u32[]{:S(2)}, u32[]{:S(2)}) %collective-permute-start.14) | collective-permute-done | bytes 1048608 | tf_op jit(solution)/shard_map/ppermute | solution.py:165
  267.4 3.5 fusion.114
  270.9 3.5 fusion.111
  280.5 78.7 %while.46 = (s32[]{:T(128)}, f32[8,1024,64]{1,2,0:T(8,128)}, f32[8,1024,64]{1,2,0:T(8,128)}, bf16[2,8,512,64]{2,3,1,0:T(8,128)(2,1)}, bf16[2,8,512,64]{2,3,1,0:T...) while((s32[]{:T(128)}, f32[8,1024,64]{1,2,0:T(8,128)}, ...), condition=%wide.region_14.15_spmd.clone, body=%wide.region_12.14_spmd.clone.sunk | while | flops 2737565696 | bytes 182567152 | solution.py:126
  280.5 3.5 fusion.230
  284.0 4.5 select_add_fusion.11
  288.5 9.6 %multiply_reduce_fusion.9 = (f32[8,512]{1,0:T(8,128)S(1)}, f32[8,512,1024]{2,1,0:T(8,128)}) fusion(f32[8,512,1024]{2,1,0:T(8,128)S(1)} %fusion.230, f32[8,512]{1,0:T(8,128)S(1)} %dynamic-slice_bitcast_fusion.2, bf16[8,1024,64]{1,2,0:T(8,128)(2,1)} %get-tuple-element.432, bf16[2,8,512,64]{2,3,1,0:T(8,128)(2,1)} %get-tuple-element.431, s32[]{:T(128)S(6)} %copy.53), kind=kOutput, calls=%fused_computation.14.clone.1 | convolution fusion | flops 553644032 | bytes 35160068 | tf_op jit(solution)/shard_map/while/body/eval_jaxpr/while/body/eval_jaxpr/hqe,hke->hqk/dot_general | solution.py:101
  298.1 10.4 %multiply_convert_fusion.9 = bf16[8,512,1024]{2,1,0:T(8,128)(2,1)} fusion(f32[8,512,1024]{2,1,0:T(8,128)} %get-tuple-element.379, f32[8,512,1024]{2,1,0:T(8,128)S(1)} %fusion.230, f32[8,512]{1,0:T(8,128)S(1)} %get-tuple-element.380, f32[8,512]{1,0:T(8,128)S(1)} %dynamic-slice_bitcast_fusion.2), kind=kLoop, calls=%fused_computation.13.clone.1 | loop fusion | flops 20971520 | bytes 41975808 | tf_op jit(solution)/shard_map/while/body/eval_jaxpr/while/body/eval_jaxpr/convert_element_type | solution.py:105
  308.5 7.0 %fusion.231 = bf16[2,8,512,64]{2,3,1,0:T(8,128)(2,1)} fusion(bf16[2,8,512,64]{2,3,1,0:T(8,128)(2,1)} %get-tuple-element.416, s32[]{:T(128)S(6)} %copy.53, bf16[8,512,1024]{2,1,0:T(8,128)(2,1)} %multiply_convert_fusion.9, bf16[8,1024,64]{1,2,0:T(8,128)(2,1)S(1)} %get-tuple-element.429), kind=kOutput, calls=%fused_computation.24.clone.1 | convolution fusion | flops 537133056 | bytes 10485764 | tf_op jit(solution)/shard_map/while/body/eval_jaxpr/while/body/eval_jaxpr/hqk,hke->hqe/dot_general | solution.py:107
  315.5 3.0 select_add_fusion.10
  318.5 3.5 fusion.230
  322.0 5.7 %select_add_fusion.11 = f32[8,1024,64]{1,2,0:T(8,128)} fusion(f32[8,1024,64]{1,2,0:T(8,128)} %get-tuple-element.415, f32[8,512,1024]{2,1,0:T(8,128)S(1)} %fusion.230, f32[8,512]{1,0:T(8,128)S(1)} %dynamic-slice_bitcast_fusion.2, pred[]{:T(512)S(6)} %compare.3, bf16[2,8,512,64]{2,3,1,0:T(8,128)(2,1)S(1)} %copy-done.6, s32[]{:T(128)S(6)} %copy.53), kind=kOutput, calls=%fused_computation.20.clone.1 | convolution fusion | flops 550502400 | bytes 21512196 | tf_op jit(solution)/shard_map/while/body/eval_jaxpr/while/body/eval_jaxpr/hqk,hqe->hke/dot_general | solution.py:117
  327.7 9.6 %multiply_reduce_fusion.9 = (f32[8,512]{1,0:T(8,128)S(1)}, f32[8,512,1024]{2,1,0:T(8,128)}) fusion(f32[8,512,1024]{2,1,0:T(8,128)S(1)} %fusion.230, f32[8,512]{1,0:T(8,128)S(1)} %dynamic-slice_bitcast_fusion.2, bf16[8,1024,64]{1,2,0:T(8,128)(2,1)} %get-tuple-element.432, bf16[2,8,512,64]{2,3,1,0:T(8,128)(2,1)} %get-tuple-element.431, s32[]{:T(128)S(6)} %copy.53), kind=kOutput, calls=%fused_computation.14.clone.1 | convolution fusion | flops 553644032 | bytes 35160068 | tf_op jit(solution)/shard_map/while/body/eval_jaxpr/while/body/eval_jaxpr/hqe,hke->hqk/dot_general | solution.py:101
  337.3 10.4 %multiply_convert_fusion.9 = bf16[8,512,1024]{2,1,0:T(8,128)(2,1)} fusion(f32[8,512,1024]{2,1,0:T(8,128)} %get-tuple-element.379, f32[8,512,1024]{2,1,0:T(8,128)S(1)} %fusion.230, f32[8,512]{1,0:T(8,128)S(1)} %get-tuple-element.380, f32[8,512]{1,0:T(8,128)S(1)} %dynamic-slice_bitcast_fusion.2), kind=kLoop, calls=%fused_computation.13.clone.1 | loop fusion | flops 20971520 | bytes 41975808 | tf_op jit(solution)/shard_map/while/body/eval_jaxpr/while/body/eval_jaxpr/convert_element_type | solution.py:105
  347.7 7.0 %fusion.231 = bf16[2,8,512,64]{2,3,1,0:T(8,128)(2,1)} fusion(bf16[2,8,512,64]{2,3,1,0:T(8,128)(2,1)} %get-tuple-element.416, s32[]{:T(128)S(6)} %copy.53, bf16[8,512,1024]{2,1,0:T(8,128)(2,1)} %multiply_convert_fusion.9, bf16[8,1024,64]{1,2,0:T(8,128)(2,1)S(1)} %get-tuple-element.429), kind=kOutput, calls=%fused_computation.24.clone.1 | convolution fusion | flops 537133056 | bytes 10485764 | tf_op jit(solution)/shard_map/while/body/eval_jaxpr/while/body/eval_jaxpr/hqk,hke->hqe/dot_general | solution.py:107
  354.7 4.5 select_add_fusion.10
  362.5 2.8 fusion.55
  367.4 3.8 convolution_convert_fusion
  374.0 5.3 fusion.147
  380.8 7.0 %fusion.135 = bf16[1,512,1024]{2,1,0:T(8,128)(2,1)} fusion(bf16[1024,4096]{1,0:T(8,128)(2,1)} %all-gather.5.cloned.1.call-done, f32[512,2048]{1,0:T(8,128)S(1)} %copy-done.16), kind=kOutput, calls=%fused_computation.169 | convolution fusion | flops 2157445120 | bytes 9437184 | tf_op jit(solution)/shard_map/lse,fe->lsf/dot_general | solution.py:180
  387.9 3.7 fusion.138
  391.7 14.0 %collective-permute-done.15 = bf16[1,512,1024]{2,1,0:T(8,128)(2,1)S(1)} collective-permute-done((bf16[1,512,1024]{2,1,0:T(8,128)(2,1)}, bf16[1,512,1024]{2,1,0:T(8,128)(2,1)S(1)}, u32[]{:S(2)}, u32[]{:S(2)}) %collective-permute-start.15) | collective-permute-done | bytes 1048608 | tf_op jit(solution)/shard_map/ppermute | solution.py:165
  405.7 4.7 fusion.93
  411.7 13.2 %collective-permute-done.11 = bf16[1,512,1024]{2,1,0:T(8,128)(2,1)} collective-permute-done((bf16[1,512,1024]{2,1,0:T(8,128)(2,1)}, bf16[1,512,1024]{2,1,0:T(8,128)(2,1)}, u32[]{:S(2)}, u32[]{:S(2)}) %collective-permute-start.11) | collective-permute-done | bytes 1048608 | tf_op jit(solution)/shard_map/ppermute | solution.py:165
  424.9 4.8 fusion.95
  440.7 3.8 collective-permute-done.19
  446.1 5.4 collective-permute-done.20
  452.5 4.6 collective-permute-done.21
  457.2 3.7 collective-permute-done.22
  462.5 5.4 copy.32
  467.8 3.5 copy.31
  477.5 77.3 %reduce-scatter.5.cloned.1.call-done = bf16[64,4096]{1,0:T(8,128)(2,1)} async-done(((bf16[1024,4096]{1,0:T(8,128)(2,1)}), bf16[64,4096]{1,0:T(8,128)(2,1)}) %reduce-scatter.5.cloned.1.call-update) | async-done | bytes 524304 | tf_op jit(solution)/shard_map/reduce_scatter | solution.py:286
  (263 shorter events, 95.6 us)
Async XLA Ops:
  7.2 17.9 %copy-start = (bf16[64,6144]{1,0:T(8,128)(2,1)S(1)}, bf16[64,6144]{1,0:T(8,128)(2,1)}, u32[]{:S(2)}) copy-start(bf16[64,6144]{1,0:T(8,128)(2,1)} %param.19) | copy-start | bytes 2359300
  7.2 24.2 %copy-start.8 = (bf16[512,1,1024]{2,0,1:T(8,128)(2,1)S(1)}, bf16[512,1,1024]{2,0,1:T(8,128)(2,1)}, u32[]{:S(2)}) copy-start(bf16[512,1,1024]{2,0,1:T(8,128)(2,1)} %param.13) | copy-start | bytes 3145732
  7.2 63.2 %all-gather.3.cloned.1.call-start = ((), (), s32[]{:S(2)}) async-start(), calls=%async_computation.2 | async-start | bytes 4456448 | tf_op jit(solution)/shard_map/all_gather | solution.py:199
  9.1 186.8 %all-gather.5.cloned.1.call-start = ((), (), s32[]{:S(2)}) async-start(), calls=%async_computation.3 | async-start | bytes 8912896 | tf_op jit(solution)/shard_map/all_gather | solution.py:202
  10.4 1.3 collective-permute-start
  11.7 4.5 collective-permute-start.1
  16.3 3.8 collective-permute-start.2
  18.4 35.9 %collective-permute-start.8 = (bf16[1,512,1024]{2,1,0:T(8,128)(2,1)}, bf16[1,512,1024]{2,1,0:T(8,128)(2,1)S(1)}, u32[]{:S(2)}, u32[]{:S(2)}) collective-permute-start(bf16[1,512,1024]{2,1,0:T(8,128)(2,1)} %bitcast.253), channel_id=1, source_target_pairs={{0,1},{1,0},{2,3},{3,2},{4,5},{5,4},{6,7},{7,6},{8,9},{9,8},{10,11... | collective-permute-start | bytes 3145736 | tf_op jit(solution)/shard_map/ppermute | solution.py:165
  20.1 4.9 collective-permute-start.3
  26.4 16.0 %collective-permute-start.4 = (f32[8,6144]{1,0:T(8,128)}, f32[8,6144]{1,0:T(8,128)S(1)}, u32[]{:S(2)}, u32[]{:S(2)}) collective-permute-start(f32[8,6144]{1,0:T(8,128)} %slice_select_fusion), channel_id=1, source_target_pairs={{0,16},{2,18},{4,20},{6,22},{8,24},{10,26},{12,28},{14,30},{16,0},... | collective-permute-start | bytes 589832 | tf_op jit(solution)/shard_map/ppermute | solution.py:139
  31.4 442.9 %reduce-scatter.3.cloned.1.call-start = ((), (), s32[]{:S(2)}) async-start(), calls=%async_computation.4 | async-start | bytes 4456448 | tf_op jit(solution)/shard_map/reduce_scatter | solution.py:299
  42.4 4.7 collective-permute-start.5
  42.5 35.5 %copy-start.38 = (f32[512]{0:T(512)}, f32[512]{0:T(512)S(1)}, u32[]{:S(2)}) copy-start(f32[512]{0:T(512)S(1)} %broadcast_multiply_fusion.2) | copy-start | bytes 6148
  47.2 5.2 collective-permute-start.6
  52.4 1.3 collective-permute-start.7
  52.5 25.5 %copy-start.42 = (f32[512]{0:T(512)}, f32[512]{0:T(512)S(1)}, u32[]{:S(2)}) copy-start(f32[512]{0:T(512)S(1)} %fusion.173) | copy-start | bytes 6148
  54.3 23.6 %copy-start.36 = (f32[1,1,1024]{2,1,0:T(1,128)}, f32[1,1,1024]{2,1,0:T(1,128)S(1)}, u32[]{:S(2)}) copy-start(f32[1,1,1024]{2,1,0:T(1,128)S(1)} %get-tuple-element.267) | copy-start | bytes 12292
  117.0 34.5 %copy-start.40 = (f32[1,1,1024]{2,1,0:T(1,128)S(1)}, f32[1,1,1024]{2,1,0:T(1,128)}, u32[]{:S(2)}) copy-start(f32[1,1,1024]{2,1,0:T(1,128)} %get-tuple-element.268) | copy-start | bytes 12292
  125.4 26.1 %collective-permute-start.9 = (bf16[1,512,1024]{2,1,0:T(8,128)(2,1)S(1)}, bf16[1,512,1024]{2,1,0:T(8,128)(2,1)S(1)}, u32[]{:S(2)}, u32[]{:S(2)}) collective-permute-start(bf16[1,512,1024]{2,1,0:T(8,128)(2,1)S(1)} %fusion.154), channel_id=1, source_target_pairs={{0,1},{1,0},{2,3},{3,2},{4,5},{5,4},{6,7},{7,6},{8,9},{9,8},{10,11... | collective-permute-start | bytes 3145736 | tf_op jit(solution)/shard_map/ppermute | solution.py:165
  127.0 47.1 %collective-permute-start.12 = (bf16[1,512,1024]{2,1,0:T(8,128)(2,1)}, bf16[1,512,1024]{2,1,0:T(8,128)(2,1)}, u32[]{:S(2)}, u32[]{:S(2)}) collective-permute-start(bf16[1,512,1024]{2,1,0:T(8,128)(2,1)} %bitcast.255), channel_id=1, source_target_pairs={{0,1},{1,0},{2,3},{3,2},{4,5},{5,4},{6,7},{7,6},{8,9},{9,8},{10,11... | collective-permute-start | bytes 3145736 | tf_op jit(solution)/shard_map/ppermute | solution.py:165
  155.5 18.6 %copy-start.34 = (f32[1,1,1024]{2,1,0:T(1,128)S(1)}, f32[1,1,1024]{2,1,0:T(1,128)}, u32[]{:S(2)}) copy-start(f32[1,1,1024]{2,1,0:T(1,128)} %get-tuple-element.263) | copy-start | bytes 12292
  158.2 37.7 %collective-permute-start.10 = (bf16[1,512,1024]{2,1,0:T(8,128)(2,1)}, bf16[1,512,1024]{2,1,0:T(8,128)(2,1)}, u32[]{:S(2)}, u32[]{:S(2)}) collective-permute-start(bf16[1,512,1024]{2,1,0:T(8,128)(2,1)} %add_convert_fusion), channel_id=1, source_target_pairs={{0,1},{1,0},{2,3},{3,2},{4,5},{5,4},{6,7},{7,6},{8,9},{9,8},{10,11... | collective-permute-start | bytes 3145736 | tf_op jit(solution)/shard_map/ppermute | solution.py:165
  209.9 24.6 %collective-permute-start.13 = (bf16[1,512,1024]{2,1,0:T(8,128)(2,1)S(1)}, bf16[1,512,1024]{2,1,0:T(8,128)(2,1)S(1)}, u32[]{:S(2)}, u32[]{:S(2)}) collective-permute-start(bf16[1,512,1024]{2,1,0:T(8,128)(2,1)S(1)} %fusion.141), channel_id=1, source_target_pairs={{0,1},{1,0},{2,3},{3,2},{4,5},{5,4},{6,7},{7,6},{8,9},{9,8},{10,11... | collective-permute-start | bytes 3145736 | tf_op jit(solution)/shard_map/ppermute | solution.py:165
  221.3 13.2 %copy-start.4 = (f32[1,512,1024]{2,1,0:T(8,128)S(1)}, f32[1,512,1024]{2,1,0:T(8,128)}, u32[]{:S(2)}) copy-start(f32[1,512,1024]{2,1,0:T(8,128)} %copy-done.3) | copy-start | bytes 6291460
  238.9 11.0 %copy-start.44 = (f32[512]{0:T(512)}, f32[512]{0:T(512)S(1)}, u32[]{:S(2)}) copy-start(f32[512]{0:T(512)S(1)} %negate_multiply_fusion.1) | copy-start | bytes 6148
  241.7 23.9 %collective-permute-start.14 = (bf16[1,512,1024]{2,1,0:T(8,128)(2,1)}, bf16[1,512,1024]{2,1,0:T(8,128)(2,1)}, u32[]{:S(2)}, u32[]{:S(2)}) collective-permute-start(bf16[1,512,1024]{2,1,0:T(8,128)(2,1)} %get-tuple-element.250), channel_id=1, source_target_pairs={{0,1},{1,0},{2,3},{3,2},{4,5},{5,4},{6,7},{7,6},{8,9},{9,8},{10,11... | collective-permute-start | bytes 3145736 | tf_op jit(solution)/shard_map/ppermute | solution.py:165
  308.5 7.0 %copy-start.1 = (bf16[8,512,1024]{2,1,0:T(8,128)(2,1)S(1)}, bf16[8,512,1024]{2,1,0:T(8,128)(2,1)}, u32[]{:S(2)}) copy-start(bf16[8,512,1024]{2,1,0:T(8,128)(2,1)} %multiply_convert_fusion.9) | copy-start | bytes 25165828 | tf_op jit(solution)/shard_map/while/body/eval_jaxpr/while
  308.5 7.0 %copy-start.2 = (bf16[2,8,512,64]{2,3,1,0:T(8,128)(2,1)S(1)}, bf16[2,8,512,64]{2,3,1,0:T(8,128)(2,1)}, u32[]{:S(2)}) copy-start(bf16[2,8,512,64]{2,3,1,0:T(8,128)(2,1)} %get-tuple-element.428) | copy-start | bytes 3145732 | tf_op jit(solution)/shard_map/while/body/eval_jaxpr/while
  347.7 7.0 %copy-start.1 = (bf16[8,512,1024]{2,1,0:T(8,128)(2,1)S(1)}, bf16[8,512,1024]{2,1,0:T(8,128)(2,1)}, u32[]{:S(2)}) copy-start(bf16[8,512,1024]{2,1,0:T(8,128)(2,1)} %multiply_convert_fusion.9) | copy-start | bytes 25165828 | tf_op jit(solution)/shard_map/while/body/eval_jaxpr/while
  347.7 7.0 %copy-start.2 = (bf16[2,8,512,64]{2,3,1,0:T(8,128)(2,1)S(1)}, bf16[2,8,512,64]{2,3,1,0:T(8,128)(2,1)}, u32[]{:S(2)}) copy-start(bf16[2,8,512,64]{2,3,1,0:T(8,128)(2,1)} %get-tuple-element.428) | copy-start | bytes 3145732 | tf_op jit(solution)/shard_map/while/body/eval_jaxpr/while
  374.0 180.8 %reduce-scatter.5.cloned.1.call-start = ((), (), s32[]{:S(2)}) async-start(), calls=%async_computation.5 | async-start | bytes 8912896 | tf_op jit(solution)/shard_map/reduce_scatter | solution.py:286
  374.0 6.8 %copy-start.16 = (f32[512,2048]{1,0:T(8,128)S(1)}, f32[512,2048]{1,0:T(8,128)}, u32[]{:S(2)}) copy-start(f32[512,2048]{1,0:T(8,128)} %copy-done.15) | copy-start | bytes 12582916
  374.0 13.9 %slice-start = ((s8[8388608]{0:T(1024)(128)(4,1)}), s8[4194304]{0:T(1024)(128)(4,1)S(1)}, s32[]{:S(2)}) async-start(s8[8388608]{0:T(1024)(128)(4,1)} %bitcast.287), calls=%async_computation.6 | async-start | bytes 8388608
  379.4 8.5 %copy-start.18 = (f32[512,2048]{1,0:T(8,128)S(1)}, f32[512,2048]{1,0:T(8,128)}, u32[]{:S(2)}) copy-start(f32[512,2048]{1,0:T(8,128)} %copy-done.17) | copy-start | bytes 12582916
  379.4 8.5 %slice-start.1 = ((s8[8388608]{0:T(1024)(128)(4,1)}), s8[4194304]{0:T(1024)(128)(4,1)S(1)}, s32[]{:S(2)}) async-start(s8[8388608]{0:T(1024)(128)(4,1)} %bitcast.287), calls=%async_computation.7 | async-start | bytes 8388608
  379.4 26.3 %collective-permute-start.15 = (bf16[1,512,1024]{2,1,0:T(8,128)(2,1)}, bf16[1,512,1024]{2,1,0:T(8,128)(2,1)S(1)}, u32[]{:S(2)}, u32[]{:S(2)}) collective-permute-start(bf16[1,512,1024]{2,1,0:T(8,128)(2,1)} %fusion.147), channel_id=1, source_target_pairs={{0,1},{1,0},{2,3},{3,2},{4,5},{5,4},{6,7},{7,6},{8,9},{9,8},{10,11... | collective-permute-start | bytes 3145736 | tf_op jit(solution)/shard_map/ppermute | solution.py:165
  387.8 37.0 %collective-permute-start.11 = (bf16[1,512,1024]{2,1,0:T(8,128)(2,1)}, bf16[1,512,1024]{2,1,0:T(8,128)(2,1)}, u32[]{:S(2)}, u32[]{:S(2)}) collective-permute-start(bf16[1,512,1024]{2,1,0:T(8,128)(2,1)} %fusion.135), channel_id=1, source_target_pairs={{0,1},{1,0},{2,3},{3,2},{4,5},{5,4},{6,7},{7,6},{8,9},{9,8},{10,11... | collective-permute-start | bytes 3145736 | tf_op jit(solution)/shard_map/ppermute | solution.py:165
  391.6 14.1 %copy-start.9 = (bf16[512,1,1024]{2,0,1:T(8,128)(2,1)S(1)}, bf16[512,1,1024]{2,0,1:T(8,128)(2,1)}, u32[]{:S(2)}) copy-start(bf16[512,1,1024]{2,0,1:T(8,128)(2,1)} %param.13) | copy-start | bytes 3145732
  391.6 14.1 %copy-start.37 = (f32[1,1,1024]{2,1,0:T(1,128)S(1)}, f32[1,1,1024]{2,1,0:T(1,128)}, u32[]{:S(2)}) copy-start(f32[1,1,1024]{2,1,0:T(1,128)} %copy-done.36) | copy-start | bytes 12292
  391.6 14.1 %copy-start.39 = (f32[512]{0:T(512)S(1)}, f32[512]{0:T(512)}, u32[]{:S(2)}) copy-start(f32[512]{0:T(512)} %copy-done.38) | copy-start | bytes 6148
  391.6 18.8 %copy-start.47 = (f32[512]{0:T(512)S(1)}, f32[512]{0:T(512)}, u32[]{:S(2)}) copy-start(f32[512]{0:T(512)} %copy-done.46) | copy-start | bytes 6148
  391.6 18.8 %copy-start.43 = (f32[512]{0:T(512)S(1)}, f32[512]{0:T(512)}, u32[]{:S(2)}) copy-start(f32[512]{0:T(512)} %copy-done.42) | copy-start | bytes 6148
  391.6 33.2 %copy-start.14 = (bf16[512,1,1024]{2,0,1:T(8,128)(2,1)S(1)}, bf16[512,1,1024]{2,0,1:T(8,128)(2,1)}, u32[]{:S(2)}) copy-start(bf16[512,1,1024]{2,0,1:T(8,128)(2,1)} %param.21) | copy-start | bytes 3145732
  391.7 33.2 %copy-start.20 = (bf16[1,512,1024]{2,1,0:T(8,128)(2,1)S(1)}, bf16[1,512,1024]{2,1,0:T(8,128)(2,1)}, u32[]{:S(2)}) copy-start(bf16[1,512,1024]{2,1,0:T(8,128)(2,1)} %copy-done.19) | copy-start | bytes 3145732
  391.7 33.2 %copy-start.21 = (bf16[1,512,1024]{2,1,0:T(8,128)(2,1)S(1)}, bf16[1,512,1024]{2,1,0:T(8,128)(2,1)}, u32[]{:S(2)}) copy-start(bf16[1,512,1024]{2,1,0:T(8,128)(2,1)} %get-tuple-element.277) | copy-start | bytes 3145732
  391.7 33.2 %copy-start.25 = (bf16[1,512,1024]{2,1,0:T(8,128)(2,1)S(1)}, bf16[1,512,1024]{2,1,0:T(8,128)(2,1)}, u32[]{:S(2)}) copy-start(bf16[1,512,1024]{2,1,0:T(8,128)(2,1)} %fusion.138) | copy-start | bytes 3145732
  391.7 33.2 %copy-start.35 = (f32[1,1,1024]{2,1,0:T(1,128)S(1)}, f32[1,1,1024]{2,1,0:T(1,128)}, u32[]{:S(2)}) copy-start(f32[1,1,1024]{2,1,0:T(1,128)} %get-tuple-element.263) | copy-start | bytes 12292
  391.7 33.2 %copy-start.45 = (f32[512]{0:T(512)S(1)}, f32[512]{0:T(512)}, u32[]{:S(2)}) copy-start(f32[512]{0:T(512)} %copy-done.44) | copy-start | bytes 6148
  405.7 19.2 %copy-start.11 = (f32[1,512,1024]{2,1,0:T(8,128)S(1)}, f32[1,512,1024]{2,1,0:T(8,128)}, u32[]{:S(2)}) copy-start(f32[1,512,1024]{2,1,0:T(8,128)} %copy-done.10) | copy-start | bytes 6291460
  410.4 14.5 %copy-start.5 = (f32[1,512,1024]{2,1,0:T(8,128)S(1)}, f32[1,512,1024]{2,1,0:T(8,128)}, u32[]{:S(2)}) copy-start(f32[1,512,1024]{2,1,0:T(8,128)} %copy-done.3) | copy-start | bytes 6291460
  429.7 38.1 %copy-start.12 = (f32[512,1,1024]{2,0,1:T(8,128)S(1)}, f32[512,1,1024]{2,0,1:T(8,128)}, u32[]{:S(2)}) copy-start(f32[512,1,1024]{2,0,1:T(8,128)} %get-tuple-element.248) | copy-start | bytes 6291460
  429.8 3.9 collective-permute-start.16
  433.7 1.3 collective-permute-start.17
  435.1 3.9 collective-permute-start.18
  439.1 5.4 collective-permute-start.19
  444.7 6.8 %collective-permute-start.20 = (bf16[8,6144]{1,0:T(8,128)(2,1)S(1)}, bf16[8,6144]{1,0:T(8,128)(2,1)S(1)}, u32[]{:S(2)}, u32[]{:S(2)}) collective-permute-start(bf16[8,6144]{1,0:T(8,128)(2,1)S(1)} %pad_maximum_fusion.8), channel_id=1, source_target_pairs={{0,16},{2,18},{4,20},{6,22},{8,24},{10,26},{12,28},{14,30},{16,0},... | collective-permute-start | bytes 294920 | tf_op jit(solution)/shard_map/ppermute | solution.py:139
  452.2 4.9 collective-permute-start.21
  457.1 3.8 collective-permute-start.22
  460.9 10.4 %collective-permute-start.23 = (f32[2,1024]{1,0:T(2,128)S(1)}, f32[2,1024]{1,0:T(2,128)S(1)}, u32[]{:S(2)}, u32[]{:S(2)}) collective-permute-start(f32[2,1024]{1,0:T(2,128)S(1)} %broadcast_select_fusion.17), channel_id=1, source_target_pairs={{0,4},{2,6},{4,0},{6,2},{8,12},{10,14},{12,8},{14,10},{16,20},{18,... | collective-permute-start | bytes 24584 | tf_op jit(solution)/shard_map/ppermute | solution.py:139
  462.5 9.0 %copy-start.31 = (bf16[8,1024]{1,0:T(8,128)(2,1)S(1)}, bf16[8,1024]{1,0:T(8,128)(2,1)}, u32[]{:S(2)}) copy-start(bf16[8,1024]{1,0:T(8,128)(2,1)} %copy-done.30) | copy-start | bytes 49156
  462.5 9.0 %copy-start.33 = (bf16[8,1024]{1,0:T(8,128)(2,1)S(1)}, bf16[8,1024]{1,0:T(8,128)(2,1)}, u32[]{:S(2)}) copy-start(bf16[8,1024]{1,0:T(8,128)(2,1)} %copy-done.32) | copy-start | bytes 49156
  462.5 11.2 %copy-start.49 = (bf16[1,1024]{1,0:T(2,128)(2,1)S(1)}, bf16[1,1024]{1,0:T(2,128)(2,1)}, u32[]{:S(2)}) copy-start(bf16[1,1024]{1,0:T(2,128)(2,1)} %param.14) | copy-start | bytes 6148
  462.5 11.2 %copy-start.50 = (f32[1,1024]{1,0:T(1,128)S(1)}, f32[1,1024]{1,0:T(1,128)}, u32[]{:S(2)}) copy-start(f32[1,1024]{1,0:T(1,128)} %get-tuple-element.239) | copy-start | bytes 12292
  471.4 2.3 collective-permute-start.24
  (27 other events, 90.1 us)
Sparse Core Ops, SparseCore 0:
  10.8 59.5 all-gather.2
  73.1 74.1 all-gather.4
  374.1 72.4 reduce-scatter.2
  451.0 103.7 reduce-scatter.4

commit v2 on v1

--- a/solution.py
+++ b/solution.py
@@ -1,9 +1,14 @@
+import functools
+
 import jax
 import jax.numpy as jnp
 from jax import lax
+from jax.experimental import pallas as pl
+from jax.experimental.pallas import tpu as pltpu
 from jax.sharding import PartitionSpec as P
 
 HEAD_DIM = 64
+KERNEL_VMEM = 40 * 2**20
 
 
 epsilon = 1e-06
@@ -22,116 +27,114 @@
     return jax.nn.gelu(inputs, approximate=True)
 
 
-def split_heads(query_key_value):
+def row_dot(left, right):
+    return lax.dot_general(left, right, (((1,), (1,)), ((), ())), preferred_element_type=jnp.float32)
+
+
+def column_dot(left, right):
+    return lax.dot_general(left, right, (((0,), (0,)), ((), ())), preferred_element_type=jnp.float32)
+
+
+def forward_kernel(score_scale, qkv_ref, attended_ref, log_ref):
+    seq_len = qkv_ref.shape[1]
+    block_rows = min(512, seq_len)
+    for head in range(2):
+        first = head * 3 * HEAD_DIM
+        key_head = qkv_ref[0, :, first + HEAD_DIM : first + 2 * HEAD_DIM]
+        value_head = qkv_ref[0, :, first + 2 * HEAD_DIM : first + 3 * HEAD_DIM]
+        for start in range(0, seq_len, block_rows):
+            rows = slice(start, start + block_rows)
+            query_block = qkv_ref[0, rows, first : first + HEAD_DIM] * score_scale
+            scores = row_dot(key_head, query_block)
+            row_max = jnp.max(scores, axis=0, keepdims=True)
+            shifted = jnp.exp(scores - row_max)
+            denom_sum = jnp.sum(shifted, axis=0, keepdims=True)
+            result = column_dot(value_head, shifted.astype(jnp.bfloat16)) / denom_sum
+            attended_ref[0, rows, head * HEAD_DIM : (head + 1) * HEAD_DIM] = result.T.astype(
+                jnp.bfloat16
+            )
+            log_ref[0, 0, head : head + 1, rows] = row_max + jnp.log(denom_sum)
+
+
+def backward_kernel(score_scale, qkv_ref, grad_ref, log_ref, out_ref):
+    seq_len = qkv_ref.shape[1]
+    block_rows = min(512, seq_len)
+    for head in range(2):
+        first = head * 3 * HEAD_DIM
+        key_head = qkv_ref[0, :, first + HEAD_DIM : first + 2 * HEAD_DIM]
+        value_head = qkv_ref[0, :, first + 2 * HEAD_DIM : first + 3 * HEAD_DIM]
+        grad_keys = jnp.zeros((seq_len, HEAD_DIM), jnp.float32)
+        grad_values = jnp.zeros((seq_len, HEAD_DIM), jnp.float32)
+        for start in range(0, seq_len, block_rows):
+            rows = slice(start, start + block_rows)
+            query_block = qkv_ref[0, rows, first : first + HEAD_DIM] * score_scale
+            grad_block = grad_ref[0, rows, head * HEAD_DIM : (head + 1) * HEAD_DIM]
+            scores = row_dot(key_head, query_block)
+            probs = jnp.exp(scores - log_ref[0, 0, head : head + 1, rows])
+            grad_probs = row_dot(value_head, grad_block)
+            delta = jnp.sum(grad_probs * probs, axis=0, keepdims=True)
+            grad_scores = (probs * (grad_probs - delta)).astype(jnp.bfloat16)
+            grad_query = column_dot(key_head, grad_scores) * score_scale
+            out_ref[0, rows, first : first + HEAD_DIM] = grad_query.T.astype(jnp.bfloat16)
+            grad_keys += jnp.dot(grad_scores, query_block, preferred_element_type=jnp.float32)
+            grad_values += jnp.dot(
+                probs.astype(jnp.bfloat16), grad_block, preferred_element_type=jnp.float32
+            )
+        out_ref[0, :, first + HEAD_DIM : first + 2 * HEAD_DIM] = grad_keys.astype(jnp.bfloat16)
+        out_ref[0, :, first + 2 * HEAD_DIM : first + 3 * HEAD_DIM] = grad_values.astype(
+            jnp.bfloat16
+        )
+
+
+def head_pair_spec(seq_len, columns):
+    return pl.BlockSpec((1, seq_len, columns), lambda latent, pair: (latent, 0, pair))
+
+
+def log_spec(seq_len):
+    return pl.BlockSpec((1, 1, 2, seq_len), lambda latent, pair: (latent, pair, 0, 0))
+
+
+def attention_forward(query_key_value, score_scale):
     latents, seq_len, features = query_key_value.shape
-    head_count = features // (3 * HEAD_DIM)
-    divided = query_key_value.reshape(latents, seq_len, head_count, 3, HEAD_DIM).transpose(
-        3, 0, 2, 1, 4
-    )
-    return (divided[0], divided[1], divided[2])
-
-
-def attention_forward(query_key_value, score_scale):
-    queries, key_heads, value_heads = split_heads(query_key_value)
-    latents, head_count, seq_len, head_width = queries.shape
-    block_rows = min(512, seq_len)
-    num_blocks = seq_len // block_rows
-
-    def per_latent(inputs):
-        query_lat, key_lat, value_lat = inputs
-
-        def per_block(query_block):
-            scores = (
-                jnp.einsum("hqe,hke->hqk", query_block, key_lat, preferred_element_type=jnp.float32)
-                * score_scale
-            )
-            row_max = jnp.max(scores, axis=-1, keepdims=True)
-            shifted = jnp.exp(scores - row_max)
-            denom_sum = jnp.sum(shifted, axis=-1, keepdims=True)
-            weights = (shifted / denom_sum).astype(jnp.bfloat16)
-            result = jnp.einsum(
-                "hqk,hke->hqe", weights, value_lat, preferred_element_type=jnp.float32
-            )
-            return (result, (row_max + jnp.log(denom_sum))[:, :, 0])
-
-        query_blocks = query_lat.reshape(head_count, num_blocks, block_rows, head_width).transpose(
-            1, 0, 2, 3
-        )
-        results, log_parts = lax.map(per_block, query_blocks)
-        results = results.transpose(1, 0, 2, 3).reshape(head_count, seq_len, head_width)
-        log_parts = log_parts.transpose(1, 0, 2).reshape(head_count, seq_len)
-        return (results, log_parts)
-
-    results, log_total = lax.map(per_latent, (queries, key_heads, value_heads))
-    attended = (
-        results.transpose(0, 2, 1, 3)
-        .reshape(latents, seq_len, head_count * head_width)
-        .astype(jnp.bfloat16)
-    )
-    return (attended, log_total)
-
-
-def attention_backward(query_key_value, attended, log_total, grad_attended, score_scale):
-    queries, key_heads, value_heads = split_heads(query_key_value)
-    latents, head_count, seq_len, head_width = queries.shape
-    grad_heads = grad_attended.reshape(latents, seq_len, head_count, head_width).transpose(
-        0, 2, 1, 3
-    )
-    block_rows = min(512, seq_len)
-    num_blocks = seq_len // block_rows
-
-    def per_latent(inputs):
-        query_lat, key_lat, value_lat, log_lat, grad_lat = inputs
-        query_blocks = query_lat.reshape(head_count, num_blocks, block_rows, head_width).transpose(
-            1, 0, 2, 3
-        )
-        grad_blocks = grad_lat.reshape(head_count, num_blocks, block_rows, head_width).transpose(
-            1, 0, 2, 3
-        )
-        log_blocks = log_lat.reshape(head_count, num_blocks, block_rows).transpose(1, 0, 2)
-
-        def advance(totals, pieces):
-            grad_keys, grad_values = totals
-            query_block, grad_block, log_block = pieces
-            scores = (
-                jnp.einsum("hqe,hke->hqk", query_block, key_lat, preferred_element_type=jnp.float32)
-                * score_scale
-            )
-            probs = jnp.exp(scores - log_block[:, :, None])
-            grad_probs = jnp.einsum(
-                "hqe,hke->hqk", grad_block, value_lat, preferred_element_type=jnp.float32
-            )
-            delta = jnp.sum(grad_probs * probs, axis=-1, keepdims=True)
-            grad_scores = (probs * (grad_probs - delta)).astype(jnp.bfloat16)
-            grad_query = (
-                jnp.einsum("hqk,hke->hqe", grad_scores, key_lat, preferred_element_type=jnp.float32)
-                * score_scale
-            )
-            grad_keys = (
-                grad_keys
-                + jnp.einsum(
-                    "hqk,hqe->hke", grad_scores, query_block, preferred_element_type=jnp.float32
-                )
-                * score_scale
-            )
-            grad_values = grad_values + jnp.einsum(
-                "hqk,hqe->hke",
-                probs.astype(jnp.bfloat16),
-                grad_block,
-                preferred_element_type=jnp.float32,
-            )
-            return ((grad_keys, grad_values), grad_query)
-
-        zeros_init = jnp.zeros((head_count, seq_len, head_width), jnp.float32)
-        (grad_keys, grad_values), grad_query = lax.scan(
-            advance, (zeros_init, zeros_init), (query_blocks, grad_blocks, log_blocks)
-        )
-        grad_query = grad_query.transpose(1, 0, 2, 3).reshape(head_count, seq_len, head_width)
-        return jnp.stack([grad_query, grad_keys, grad_values], 0)
-
-    gradients = lax.map(per_latent, (queries, key_heads, value_heads, log_total, grad_heads))
-    seq_first = gradients.transpose(0, 3, 2, 1, 4)
-    return seq_first.reshape(latents, seq_len, head_count * 3 * head_width).astype(jnp.bfloat16)
+    pairs = features // (6 * HEAD_DIM)
+    work = latents * pairs * 2 * seq_len * seq_len
+    return pl.pallas_call(
+        functools.partial(forward_kernel, score_scale),
+        grid=(latents, pairs),
+        in_specs=[head_pair_spec(seq_len, 6 * HEAD_DIM)],
+        out_specs=[head_pair_spec(seq_len, 2 * HEAD_DIM), log_spec(seq_len)],
+        out_shape=[
+            jax.ShapeDtypeStruct((latents, seq_len, features // 3), jnp.bfloat16),
+            jax.ShapeDtypeStruct((latents, pairs, 2, seq_len), jnp.float32),
+        ],
+        compiler_params=pltpu.CompilerParams(vmem_limit_bytes=KERNEL_VMEM),
+        cost_estimate=pl.CostEstimate(
+            flops=4 * work * HEAD_DIM * 4, bytes_accessed=8 * latents * seq_len * features // 3, transcendentals=work
+        ),
+        name="attention_forward",
+    )(query_key_value)
+
+
+def attention_backward(query_key_value, log_total, grad_attended, score_scale):
+    latents, seq_len, features = query_key_value.shape
+    pairs = features // (6 * HEAD_DIM)
+    work = latents * pairs * 2 * seq_len * seq_len
+    return pl.pallas_call(
+        functools.partial(backward_kernel, score_scale),
+        grid=(latents, pairs),
+        in_specs=[
+            head_pair_spec(seq_len, 6 * HEAD_DIM),
+            head_pair_spec(seq_len, 2 * HEAD_DIM),
+            log_spec(seq_len),
+        ],
+        out_specs=head_pair_spec(seq_len, 6 * HEAD_DIM),
+        out_shape=jax.ShapeDtypeStruct((latents, seq_len, features), jnp.bfloat16),
+        compiler_params=pltpu.CompilerParams(vmem_limit_bytes=KERNEL_VMEM),
+        cost_estimate=pl.CostEstimate(
+            flops=10 * work * HEAD_DIM * 4, bytes_accessed=14 * latents * seq_len * features // 3, transcendentals=work
+        ),
+        name="attention_backward",
+    )(query_key_value, grad_attended, log_total)
 
 
 def dp_partner(value, bit):
@@ -208,6 +211,7 @@
     own_cotangent = cotangent.transpose(1, 0, 2)
     token_parts = spread(own_tokens)
     cotangent_parts = spread(own_cotangent)
+    token_parts, cotangent_parts = lax.optimization_barrier((token_parts, cotangent_parts))
     cond_value = cond.astype(jnp.float32)
     cond_act = jax.nn.silu(cond_value).astype(jnp.bfloat16)
     all_cond_act = gather_small(cond_act)
@@ -291,14 +295,15 @@
         "lsf,lse->fe", full_grad_branch, attended, preferred_element_type=jnp.float32
     ).astype(jnp.bfloat16)
     grad_query_key_value = attention_backward(
-        query_key_value, attended, log_total, grad_attended, score_scale
+        query_key_value, log_total, grad_attended, score_scale
     )
     grad_qkv = jnp.einsum(
         "lsd,lsw->dw", full_normed1, grad_query_key_value, preferred_element_type=jnp.float32
     ).astype(jnp.bfloat16)
-    first_grads = lax.psum_scatter(
-        jnp.concatenate([grad_qkv, grad_out], axis=1), "dp", scatter_dimension=0, tiled=True
-    )
+    first_grads, second_grads = lax.optimization_barrier(
+        (jnp.concatenate([grad_qkv, grad_out], axis=1), second_grads)
+    )
+    first_grads = lax.psum_scatter(first_grads, "dp", scatter_dimension=0, tiled=True)
     grad_parts = (
         [grad_query_key_value[:, :own_count], grad_query_key_value[:, own_count:]]
         if len(token_parts) == 2

time: 574 us -> 446 us (0.78)
  matrix products: 160 us -> 68.8 us
  Pallas kernels: 0 us -> 44.7 us
  other arithmetic: 75.9 us -> 42.8 us
  local copies, waits for them, and re-layouts: 46.5 us -> 13.9 us
  waiting for transfers between devices: 236 us -> 218 us
  starting transfers between devices: 30.8 us -> 37.3 us
    dot_general x14 -> x0, matrix products: 73.6 us -> none  [the longest x2 19.3 us: advance(): jnp.einsum('hqe,hke->hqk', grad_block, value_lat, preferred_element_type=...]
    reduce_scatter x1, waiting for transfers between devices: 77.3 us -> 14.8 us  [body(): lax.psum_scatter(second_grads, 'dp', scatter_dimension=0, tiled=True)]
    pallas_call x0 -> x2, Pallas kernels: none -> 44.7 us  [the longest x1 27.3 us: attention_backward(): pl.pallas_call(functools.partial(backward_kernel, score_scale), grid=(lat...]
    reduce_scatter x1, waiting for transfers between devices: 0.01 us -> 42.2 us  [body(): lax.psum_scatter(first_grads, 'dp', scatter_dimension=0, tiled=True)]
    ppermute x9, waiting for transfers between devices: 100 us -> 126 us  [swap(): return lax.ppermute(value, 'tensor', [(0, 1), (1, 0)])]
    convert_element_type x3 -> x1, other arithmetic: 23.6 us -> 1.34 us  [body(): grad_branch = (grad_middle * gate1).astype(jnp.bfloat16)]
    all_gather x1, waiting for transfers between devices: 13.2 us -> 0.01 us  [body(): lax.all_gather(jnp.concatenate([qkv_weight, out_weight], axis=1), 'dp', a...]
    dot_general x8, matrix products: 32.8 us -> 20.5 us  [term(): jnp.einsum('lse,fe->lsf', part, weight, preferred_element_type=jnp.float32)]
  transfers between devices with their start and end apart: 29 -> 29, of which waited for: 24 -> 22; matrix products, arithmetic and copies ran while one was open for 26% -> 21% of each run, Pallas kernels for 0% -> 10%
where the time goes in v2:
time: 446 us; the launch traced here: 441 us
  waiting for transfers between devices  218 us (49%)
  matrix products  68.8 us (15%)
  Pallas kernels  44.7 us (10%)
  other arithmetic  42.8 us (10%)
  starting transfers between devices  37.3 us (8%)
  between operations  15 us (3%)
  local copies, waits for them, and re-layouts  13.9 us (3%)
    ppermute x9, waiting for transfers between devices, swap(): return lax.ppermute(value, 'tensor', [(0, 1), (1, 0)])  126 us
    reduce_scatter x1, waiting for transfers between devices, body(): lax.psum_scatter(first_grads, 'dp', scatter_dimension=0, tiled=True)  42.2 us
    ppermute x16, waiting for transfers between devices, dp_partner(): lax.ppermute(value, 'dp', [(index, index ^ bit) for index in range(size)])  35 us
    pallas_call x1, Pallas kernels, attention_backward(): pl.pallas_call(functools.partial(backward_kernel, score_scale), grid=(lat...  27.3 us
    ppermute x16, starting transfers between devices, dp_partner(): lax.ppermute(value, 'dp', [(index, index ^ bit) for index in range(size)])  24.9 us
    dot_general x8, matrix products, term(): jnp.einsum('lse,fe->lsf', part, weight, preferred_element_type=jnp.float32)  20.5 us
    pallas_call x1, Pallas kernels, attention_forward(): pl.pallas_call(functools.partial(forward_kernel, score_scale), grid=(late...  17.4 us
    reduce_scatter x1, waiting for transfers between devices, body(): lax.psum_scatter(second_grads, 'dp', scatter_dimension=0, tiled=True)  14.8 us
  transfers between devices with their start and end apart: 29, of which 22 were waited for; matrix products, arithmetic and copies ran while one was open for 21% of the time, Pallas kernels for 10%

profile of v2, /device:TPU:0, one launch (start us, length us, event | category | flops | bytes accessed | tf_op | source)
XLA Modules:
  0.0 440.6 jit_solution(8274811776489829563)
XLA Ops:
  7.3 1.8 pad_maximum_fusion.4
  11.8 2.9 collective-permute-start.1
  14.7 1.6 collective-permute-done.1
  16.3 2.2 collective-permute-start.2
  18.5 1.6 collective-permute-done.2
  20.2 3.1 collective-permute-start.3
  26.1 3.1 collective-permute-start.4
  29.3 1.9 pad_maximum_fusion.3
  31.2 11.1 %collective-permute-done.4 = f32[8,6144]{1,0:T(8,128)S(1)} collective-permute-done((f32[8,6144]{1,0:T(8,128)}, f32[8,6144]{1,0:T(8,128)S(1)}, u32[]{:S(2)}, u32[]{:S(2)}) %collective-permute-start.4) | collective-permute-done | bytes 196640 | tf_op jit(solution)/shard_map/ppermute | solution.py:142
  42.5 4.6 %collective-permute-done.5 = f32[4,6144]{1,0:T(4,128)S(1)} collective-permute-done((f32[4,6144]{1,0:T(4,128)S(1)}, f32[4,6144]{1,0:T(4,128)S(1)}, u32[]{:S(2)}, u32[]{:S(2)}) %collective-permute-start.5) | collective-permute-done | bytes 98336 | tf_op jit(solution)/shard_map/ppermute | solution.py:142
  47.2 1.6 collective-permute-start.6
  48.8 3.6 collective-permute-done.6
  52.5 1.6 collective-permute-start.8
  54.7 23.9 %collective-permute-done.8 = bf16[1,512,1024]{2,1,0:T(8,128)(2,1)S(1)} collective-permute-done((bf16[1,512,1024]{2,1,0:T(8,128)(2,1)S(1)}, bf16[1,512,1024]{2,1,0:T(8,128)(2,1)S(1)}, u32[]{:S(2)}, u32[]{:S(2)}) %collective-permute-start.8) | collective-permute-done | bytes 1048608 | tf_op jit(solution)/shard_map/ppermute | solution.py:168
  78.5 22.1 %collective-permute-done.9 = bf16[1,512,1024]{2,1,0:T(8,128)(2,1)} collective-permute-done((bf16[1,512,1024]{2,1,0:T(8,128)(2,1)S(1)}, bf16[1,512,1024]{2,1,0:T(8,128)(2,1)}, u32[]{:S(2)}, u32[]{:S(2)}) %collective-permute-start.9) | collective-permute-done | bytes 1048608 | tf_op jit(solution)/shard_map/ppermute | solution.py:168
  101.9 1.8 fusion.60
  104.7 6.6 %fusion.22.qkv_ref = bf16[1,1024,1536]{2,1,0:T(8,128)(2,1)S(1)} fusion(bf16[1024,2048]{1,0:T(8,128)(2,1)} %all-gather.3.cloned.1.call-done, bf16[1,512,1024]{2,1,0:T(8,128)(2,1)} %get-tuple-element.78, bf16[1,512,1024]{2,1,0:T(8,128)(2,1)S(1)} %get-tuple-element.77), kind=kOutput, calls=%fused_computation.35 | convolution fusion | flops 3226992640 | bytes 8388608 | tf_op jit(solution)/shard_map/lsd,dw->lsw/dot_general | solution.py:237
  111.4 17.4 %attention_forward.1 = (bf16[1,1024,512]{2,1,0:T(8,128)(2,1)S(1)}, f32[1,4,2,1024]{3,2,1,0:T(2,128)S(1)}) custom-call(bf16[1,1024,1536]{2,1,0:T(8,128)(2,1)S(1)} %fusion.22.qkv_ref), custom_call_target="tpu_custom_call" | custom-call | flops 8589934592 | bytes 4194304 | tf_op jit(solution)/shard_map/attention_forward/pallas_call | solution.py:101
  130.8 22.8 %collective-permute-done.10 = bf16[1,512,1024]{2,1,0:T(8,128)(2,1)S(1)} collective-permute-done((bf16[1,512,1024]{2,1,0:T(8,128)(2,1)S(1)}, bf16[1,512,1024]{2,1,0:T(8,128)(2,1)S(1)}, u32[]{:S(2)}, u32[]{:S(2)}) %collective-permute-start.10) | collective-permute-done | bytes 1048608 | tf_op jit(solution)/shard_map/ppermute | solution.py:168
  154.6 2.0 fusion.162
  158.8 3.2 multiply_convert_fusion.4
  162.0 18.7 %collective-permute-done.11 = bf16[1,512,1024]{2,1,0:T(8,128)(2,1)} collective-permute-done((bf16[1,512,1024]{2,1,0:T(8,128)(2,1)S(1)}, bf16[1,512,1024]{2,1,0:T(8,128)(2,1)}, u32[]{:S(2)}, u32[]{:S(2)}) %collective-permute-start.11) | collective-permute-done | bytes 1048608 | tf_op jit(solution)/shard_map/ppermute | solution.py:168
  180.7 5.0 %fusion.40 = f32[512,2048]{1,0:T(8,128)S(1)} fusion(bf16[1024,4096]{1,0:T(8,128)(2,1)} %all-gather.5.cloned.1.call-done, bf16[1,512,1024]{2,1,0:T(8,128)(2,1)} %collective-permute-done.11), kind=kOutput, calls=%fused_computation.58 | convolution fusion | flops 2147483648 | bytes 9437184 | tf_op jit(solution)/shard_map/lsd,dw->lsw/dot_general | solution.py:250
  187.7 5.1 %fusion.13 = bf16[512,2048]{1,0:T(8,128)(2,1)S(1)} fusion(f32[512,2048]{1,0:T(8,128)S(1)} %fusion.40, bf16[1024,4096]{1,0:T(8,128)(2,1)S(1)} %copy-done.39, bf16[1,512,1024]{2,1,0:T(8,128)(2,1)S(1)} %copy-done.23), kind=kOutput, calls=%fused_computation.19 | convolution fusion | flops 2168455168 | bytes 11534336 | tf_op jit(solution)/shard_map/lsf,fe->lse/dot_general | solution.py:263
  192.8 2.4 fusion.110
  195.2 1.6 collective-permute-start.13
  196.8 2.4 fusion.42
  201.2 6.3 %fusion.20 = bf16[1024,2048]{1,0:T(8,128)(2,1)} fusion(bf16[1,512,2048]{2,1,0:T(8,128)(2,1)S(1)} %fusion.160, bf16[1,512,2048]{2,1,0:T(8,128)(2,1)S(1)} %fusion.159, bf16[1,512,1024]{2,1,0:T(8,128)(2,1)S(1)} %copy-done.23, bf16[1,512,1024]{2,1,0:T(8,128)(2,1)S(1)} %copy-done.22), kind=kOutput, calls=%fused_computation.31 | convolution fusion | flops 4309647360 | bytes 10485760 | tf_op jit(solution)/shard_map/lsf,lse->fe/dot_general | solution.py:268
  207.4 4.9 %fusion.6 = bf16[512,2048]{1,0:T(8,128)(2,1)S(1)} fusion(f32[512,2048]{1,0:T(8,128)S(1)} %fusion.42, bf16[1024,4096]{1,0:T(8,128)(2,1)S(1)} %copy-done.39, bf16[1,512,1024]{2,1,0:T(8,128)(2,1)S(1)} %copy-done.22), kind=kOutput, calls=%fused_computation.12 | convolution fusion | flops 2168455168 | bytes 11534336 | tf_op jit(solution)/shard_map/lsf,fe->lse/dot_general | solution.py:263
  212.3 5.1 %collective-permute-done.13 = bf16[1,512,1024]{2,1,0:T(8,128)(2,1)S(1)} collective-permute-done((bf16[1,512,1024]{2,1,0:T(8,128)(2,1)S(1)}, bf16[1,512,1024]{2,1,0:T(8,128)(2,1)S(1)}, u32[]{:S(2)}, u32[]{:S(2)}) %collective-permute-start.13) | collective-permute-done | bytes 1048608 | tf_op jit(solution)/shard_map/ppermute | solution.py:168
  217.4 3.0 multiply_reduce_fusion
  224.0 1.7 collective-permute-start.14
  225.7 7.4 %fusion.21 = bf16[1024,2048]{1,0:T(8,128)(2,1)} fusion(bf16[1,512,2048]{2,1,0:T(8,128)(2,1)S(1)} %bitcast.173, bf16[1,512,2048]{2,1,0:T(8,128)(2,1)S(1)} %bitcast.174, bf16[1,512,1024]{2,1,0:T(8,128)(2,1)} %collective-permute-done.11, bf16[1,512,1024]{2,1,0:T(8,128)(2,1)S(1)} %copy-done.25), kind=kOutput, calls=%fused_computation.32 | convolution fusion | flops 4309647360 | bytes 10485760 | tf_op jit(solution)/shard_map/lsd,lse->de/dot_general | solution.py:274
  233.1 7.8 %pad_maximum_fusion = bf16[1024,4096]{1,0:T(8,128)(2,1)} fusion(bf16[1024,2048]{1,0:T(8,128)(2,1)} %fusion.20, bf16[1024,2048]{1,0:T(8,128)(2,1)} %fusion.21), kind=kLoop, calls=%fused_computation | loop fusion | flops 16777216 | bytes 16777216 | tf_op jit(solution)/shard_map/concatenate | solution.py:280
  240.9 4.8 %collective-permute-done.14 = bf16[1,512,1024]{2,1,0:T(8,128)(2,1)} collective-permute-done((bf16[1,512,1024]{2,1,0:T(8,128)(2,1)}, bf16[1,512,1024]{2,1,0:T(8,128)(2,1)}, u32[]{:S(2)}, u32[]{:S(2)}) %collective-permute-start.14) | collective-permute-done | bytes 1048608 | tf_op jit(solution)/shard_map/ppermute | solution.py:168
  245.7 3.0 pad_maximum_fusion.2
  248.8 3.2 fusion.122.grad_ref
  252.1 27.3 %attention_backward.1 = bf16[1,1024,1536]{2,1,0:T(8,128)(2,1)S(1)} custom-call(bf16[1,1024,1536]{2,1,0:T(8,128)(2,1)S(1)} %copy-done.2, bf16[1,1024,512]{2,1,0:T(8,128)(2,1)S(1)} %fusion.122.grad_ref, f32[1,4,2,1024]{3,2,1,0:T(2,128)S(1)} %get-tuple-element.25.log_ref), custom_call_target="tpu_custom_call" | custom-call | flops 21474836480 | bytes 7340032 | tf_op jit(solution)/shard_map/attention_backward/pallas_call | solution.py:122
  279.4 1.8 fusion.116
  281.3 1.8 collective-permute-start.15
  283.1 5.6 %fusion.104 = bf16[1,512,1024]{2,1,0:T(8,128)(2,1)S(1)} fusion(bf16[1024,4096]{1,0:T(8,128)(2,1)} %all-gather.5.cloned.1.call-done, f32[512,2048]{1,0:T(8,128)S(1)} %copy-done.15), kind=kOutput, calls=%fused_computation.130 | convolution fusion | flops 2157445120 | bytes 9437184 | tf_op jit(solution)/shard_map/lse,fe->lsf/dot_general | solution.py:183
  289.4 2.7 fusion.107
  292.1 15.3 %collective-permute-done.15 = bf16[1,512,1024]{2,1,0:T(8,128)(2,1)S(1)} collective-permute-done((bf16[1,512,1024]{2,1,0:T(8,128)(2,1)S(1)}, bf16[1,512,1024]{2,1,0:T(8,128)(2,1)S(1)}, u32[]{:S(2)}, u32[]{:S(2)}) %collective-permute-start.15) | collective-permute-done | bytes 1048608 | tf_op jit(solution)/shard_map/ppermute | solution.py:168
  307.5 2.2 fusion.62
  311.0 13.4 %collective-permute-done.12 = bf16[1,512,1024]{2,1,0:T(8,128)(2,1)S(1)} collective-permute-done((bf16[1,512,1024]{2,1,0:T(8,128)(2,1)S(1)}, bf16[1,512,1024]{2,1,0:T(8,128)(2,1)S(1)}, u32[]{:S(2)}, u32[]{:S(2)}) %collective-permute-start.12) | collective-permute-done | bytes 1048608 | tf_op jit(solution)/shard_map/ppermute | solution.py:168
  324.4 3.5 fusion.61
  327.9 1.8 collective-permute-start.16
  329.7 3.9 convolution_convert_fusion
  336.7 2.6 pad_maximum_fusion.1
  339.8 14.8 %reduce-scatter.3.cloned.1.call-done = bf16[64,4096]{1,0:T(8,128)(2,1)} async-done(((bf16[1024,4096]{1,0:T(8,128)(2,1)}), bf16[64,4096]{1,0:T(8,128)(2,1)}) %reduce-scatter.3.cloned.1.call-update) | async-done | bytes 524304 | tf_op jit(solution)/shard_map/reduce_scatter | solution.py:290
  354.7 1.8 collective-permute-start.19
  356.5 2.4 collective-permute-done.19
  359.1 2.2 collective-permute-start.20
  361.3 3.3 collective-permute-done.20
  365.3 2.3 collective-permute-start.21
  367.7 2.5 collective-permute-done.21
  370.2 1.9 collective-permute-start.22
  372.2 1.9 collective-permute-done.22
  374.1 1.5 collective-permute-start.23
  375.6 5.2 %copy.20 = f32[512,1,1024]{2,1,0:T(1,128)} copy(f32[512,1,1024]{2,0,1:T(8,128)} %get-tuple-element.54) | data formatting | bytes 4194304
  380.8 3.5 copy.19
  384.4 1.6 fusion.139
  388.3 42.2 %reduce-scatter.5.cloned.1.call-done = bf16[64,2048]{1,0:T(8,128)(2,1)} async-done(((bf16[1024,2048]{1,0:T(8,128)(2,1)}), bf16[64,2048]{1,0:T(8,128)(2,1)}) %reduce-scatter.5.cloned.1.call-update) | async-done | bytes 262160 | tf_op jit(solution)/shard_map/reduce_scatter | solution.py:306
  432.0 1.7 slice_convert_fusion.2
  (184 shorter events, 31.9 us)
Async XLA Ops:
  7.2 17.9 %copy-start = (bf16[64,6144]{1,0:T(8,128)(2,1)S(1)}, bf16[64,6144]{1,0:T(8,128)(2,1)}, u32[]{:S(2)}) copy-start(bf16[64,6144]{1,0:T(8,128)(2,1)} %param.15) | copy-start | bytes 2359300
  7.2 45.3 %copy-start.6 = (bf16[512,1,1024]{2,0,1:T(8,128)(2,1)S(1)}, bf16[512,1,1024]{2,0,1:T(8,128)(2,1)}, u32[]{:S(2)}) copy-start(bf16[512,1,1024]{2,0,1:T(8,128)(2,1)} %param.9) | copy-start | bytes 3145732
  7.2 46.9 %copy-start.9 = (bf16[512,1,1024]{2,0,1:T(8,128)(2,1)S(1)}, bf16[512,1,1024]{2,0,1:T(8,128)(2,1)}, u32[]{:S(2)}) copy-start(bf16[512,1,1024]{2,0,1:T(8,128)(2,1)} %param.17) | copy-start | bytes 3145732
  7.2 96.5 %all-gather.3.cloned.1.call-start = ((), (), s32[]{:S(2)}) async-start(), calls=%async_computation.2 | async-start | bytes 4456448 | tf_op jit(solution)/shard_map/all_gather | solution.py:202
  9.1 171.5 %all-gather.5.cloned.1.call-start = ((), (), s32[]{:S(2)}) async-start(), calls=%async_computation.3 | async-start | bytes 8912896 | tf_op jit(solution)/shard_map/all_gather | solution.py:205
  10.5 1.3 collective-permute-start
  11.8 4.5 %collective-permute-start.1 = (bf16[2,1024]{1,0:T(2,128)(2,1)S(1)}, bf16[2,1024]{1,0:T(2,128)(2,1)S(1)}, u32[]{:S(2)}, u32[]{:S(2)}) collective-permute-start(bf16[2,1024]{1,0:T(2,128)(2,1)S(1)} %pad_maximum_fusion.13), channel_id=1, source_target_pairs={{0,4},{2,6},{4,0},{6,2},{8,12},{10,14},{12,8},{14,10},{16,20},{18,... | collective-permute-start | bytes 12296 | tf_op jit(solution)/shard_map/ppermute | solution.py:142
  16.3 3.8 collective-permute-start.2
  20.2 4.9 %collective-permute-start.3 = (bf16[8,1024]{1,0:T(8,128)(2,1)S(1)}, bf16[8,1024]{1,0:T(8,128)(2,1)S(1)}, u32[]{:S(2)}, u32[]{:S(2)}) collective-permute-start(bf16[8,1024]{1,0:T(8,128)(2,1)S(1)} %pad_maximum_fusion.11), channel_id=1, source_target_pairs={{0,16},{2,18},{4,20},{6,22},{8,24},{10,26},{12,28},{14,30},{16,0},... | collective-permute-start | bytes 49160 | tf_op jit(solution)/shard_map/ppermute | solution.py:142
  25.1 75.9 %copy-start.33 = (bf16[8,1024]{1,0:T(8,128)(2,1)}, bf16[8,1024]{1,0:T(8,128)(2,1)S(1)}, u32[]{:S(2)}) copy-start(bf16[8,1024]{1,0:T(8,128)(2,1)S(1)} %get-tuple-element.67) | copy-start | bytes 49156
  25.1 75.9 %copy-start.35 = (bf16[8,1024]{1,0:T(8,128)(2,1)}, bf16[8,1024]{1,0:T(8,128)(2,1)S(1)}, u32[]{:S(2)}) copy-start(bf16[8,1024]{1,0:T(8,128)(2,1)S(1)} %get-tuple-element.68) | copy-start | bytes 49156
  26.1 16.2 %collective-permute-start.4 = (f32[8,6144]{1,0:T(8,128)}, f32[8,6144]{1,0:T(8,128)S(1)}, u32[]{:S(2)}, u32[]{:S(2)}) collective-permute-start(f32[8,6144]{1,0:T(8,128)} %slice_select_fusion), channel_id=1, source_target_pairs={{0,16},{2,18},{4,20},{6,22},{8,24},{10,26},{12,28},{14,30},{16,0},... | collective-permute-start | bytes 589832 | tf_op jit(solution)/shard_map/ppermute | solution.py:142
  31.1 323.5 %reduce-scatter.3.cloned.1.call-start = ((), (), s32[]{:S(2)}) async-start(), calls=%async_computation.4 | async-start | bytes 8912896 | tf_op jit(solution)/shard_map/reduce_scatter | solution.py:290
  42.4 4.7 %collective-permute-start.5 = (f32[4,6144]{1,0:T(4,128)S(1)}, f32[4,6144]{1,0:T(4,128)S(1)}, u32[]{:S(2)}, u32[]{:S(2)}) collective-permute-start(f32[4,6144]{1,0:T(4,128)S(1)} %slice_select_fusion.1), channel_id=1, source_target_pairs={{0,8},{2,10},{4,12},{6,14},{8,0},{10,2},{12,4},{14,6},{16,24},{18,... | collective-permute-start | bytes 294920 | tf_op jit(solution)/shard_map/ppermute | solution.py:142
  47.2 5.2 %collective-permute-start.6 = (f32[2,6144]{1,0:T(2,128)S(1)}, f32[2,6144]{1,0:T(2,128)S(1)}, u32[]{:S(2)}, u32[]{:S(2)}) collective-permute-start(f32[2,6144]{1,0:T(2,128)S(1)} %broadcast_select_fusion.6), channel_id=1, source_target_pairs={{0,4},{2,6},{4,0},{6,2},{8,12},{10,14},{12,8},{14,10},{16,20},{18,... | collective-permute-start | bytes 147464 | tf_op jit(solution)/shard_map/ppermute | solution.py:142
  52.4 2.2 collective-permute-start.7
  52.5 26.0 %collective-permute-start.8 = (bf16[1,512,1024]{2,1,0:T(8,128)(2,1)S(1)}, bf16[1,512,1024]{2,1,0:T(8,128)(2,1)S(1)}, u32[]{:S(2)}, u32[]{:S(2)}) collective-permute-start(bf16[1,512,1024]{2,1,0:T(8,128)(2,1)S(1)} %bitcast.146), channel_id=1, source_target_pairs={{0,1},{1,0},{2,3},{3,2},{4,5},{5,4},{6,7},{7,6},{8,9},{9,8},{10,11... | collective-permute-start | bytes 3145736 | tf_op jit(solution)/shard_map/ppermute | solution.py:168
  54.1 46.5 %collective-permute-start.9 = (bf16[1,512,1024]{2,1,0:T(8,128)(2,1)S(1)}, bf16[1,512,1024]{2,1,0:T(8,128)(2,1)}, u32[]{:S(2)}, u32[]{:S(2)}) collective-permute-start(bf16[1,512,1024]{2,1,0:T(8,128)(2,1)S(1)} %bitcast.150), channel_id=1, source_target_pairs={{0,1},{1,0},{2,3},{3,2},{4,5},{5,4},{6,7},{7,6},{8,9},{9,8},{10,11... | collective-permute-start | bytes 3145736 | tf_op jit(solution)/shard_map/ppermute | solution.py:168
  111.3 17.4 %copy-start.1 = (bf16[1,1024,1536]{2,1,0:T(8,128)(2,1)}, bf16[1,1024,1536]{2,1,0:T(8,128)(2,1)S(1)}, u32[]{:S(2)}) copy-start(bf16[1,1024,1536]{2,1,0:T(8,128)(2,1)S(1)} %fusion.22.qkv_ref) | copy-start | bytes 9437188
  111.3 17.4 %copy-start.30 = (bf16[1024,2048]{1,0:T(8,128)(2,1)S(1)}, bf16[1024,2048]{1,0:T(8,128)(2,1)}, u32[]{:S(2)}) copy-start(bf16[1024,2048]{1,0:T(8,128)(2,1)} %all-gather.3.cloned.1.call-done) | copy-start | bytes 12582916
  129.5 24.1 %collective-permute-start.10 = (bf16[1,512,1024]{2,1,0:T(8,128)(2,1)S(1)}, bf16[1,512,1024]{2,1,0:T(8,128)(2,1)S(1)}, u32[]{:S(2)}, u32[]{:S(2)}) collective-permute-start(bf16[1,512,1024]{2,1,0:T(8,128)(2,1)S(1)} %fusion.126), channel_id=1, source_target_pairs={{0,1},{1,0},{2,3},{3,2},{4,5},{5,4},{6,7},{7,6},{8,9},{9,8},{10,11... | collective-permute-start | bytes 3145736 | tf_op jit(solution)/shard_map/ppermute | solution.py:168
  156.6 5.4 %copy-start.3 = (f32[1,512,1024]{2,1,0:T(8,128)}, f32[1,512,1024]{2,1,0:T(8,128)S(1)}, u32[]{:S(2)}) copy-start(f32[1,512,1024]{2,1,0:T(8,128)S(1)} %get-tuple-element.51) | copy-start | bytes 6291460
  157.4 4.6 %copy-start.24 = (bf16[1,512,1024]{2,1,0:T(8,128)(2,1)}, bf16[1,512,1024]{2,1,0:T(8,128)(2,1)S(1)}, u32[]{:S(2)}) copy-start(bf16[1,512,1024]{2,1,0:T(8,128)(2,1)S(1)} %add_convert_fusion) | copy-start | bytes 3145732
  157.4 23.3 %collective-permute-start.11 = (bf16[1,512,1024]{2,1,0:T(8,128)(2,1)S(1)}, bf16[1,512,1024]{2,1,0:T(8,128)(2,1)}, u32[]{:S(2)}, u32[]{:S(2)}) collective-permute-start(bf16[1,512,1024]{2,1,0:T(8,128)(2,1)S(1)} %add_convert_fusion), channel_id=1, source_target_pairs={{0,1},{1,0},{2,3},{3,2},{4,5},{5,4},{6,7},{7,6},{8,9},{9,8},{10,11... | collective-permute-start | bytes 3145736 | tf_op jit(solution)/shard_map/ppermute | solution.py:168
  180.7 7.0 %copy-start.39 = (bf16[1024,4096]{1,0:T(8,128)(2,1)S(1)}, bf16[1024,4096]{1,0:T(8,128)(2,1)}, u32[]{:S(2)}) copy-start(bf16[1024,4096]{1,0:T(8,128)(2,1)} %all-gather.5.cloned.1.call-done) | copy-start | bytes 25165828
  192.8 4.0 copy-start.25
  195.2 22.3 %collective-permute-start.13 = (bf16[1,512,1024]{2,1,0:T(8,128)(2,1)S(1)}, bf16[1,512,1024]{2,1,0:T(8,128)(2,1)S(1)}, u32[]{:S(2)}, u32[]{:S(2)}) collective-permute-start(bf16[1,512,1024]{2,1,0:T(8,128)(2,1)S(1)} %fusion.110), channel_id=1, source_target_pairs={{0,1},{1,0},{2,3},{3,2},{4,5},{5,4},{6,7},{7,6},{8,9},{9,8},{10,11... | collective-permute-start | bytes 3145736 | tf_op jit(solution)/shard_map/ppermute | solution.py:168
  199.1 8.3 %copy-start.16 = (f32[512,2048]{1,0:T(8,128)}, f32[512,2048]{1,0:T(8,128)S(1)}, u32[]{:S(2)}) copy-start(f32[512,2048]{1,0:T(8,128)S(1)} %fusion.42) | copy-start | bytes 12582916
  207.4 10.0 %copy-start.4 = (f32[1,512,1024]{2,1,0:T(8,128)S(1)}, f32[1,512,1024]{2,1,0:T(8,128)}, u32[]{:S(2)}) copy-start(f32[1,512,1024]{2,1,0:T(8,128)} %copy-done.3) | copy-start | bytes 6291460
  220.4 2.2 copy-start.11
  224.0 21.7 %collective-permute-start.14 = (bf16[1,512,1024]{2,1,0:T(8,128)(2,1)}, bf16[1,512,1024]{2,1,0:T(8,128)(2,1)}, u32[]{:S(2)}, u32[]{:S(2)}) collective-permute-start(bf16[1,512,1024]{2,1,0:T(8,128)(2,1)} %multiply_convert_fusion.2), channel_id=1, source_target_pairs={{0,1},{1,0},{2,3},{3,2},{4,5},{5,4},{6,7},{7,6},{8,9},{9,8},{10,11... | collective-permute-start | bytes 3145736 | tf_op jit(solution)/shard_map/ppermute | solution.py:168
  248.8 181.7 %reduce-scatter.5.cloned.1.call-start = ((), (), s32[]{:S(2)}) async-start(), calls=%async_computation.5 | async-start | bytes 4456448 | tf_op jit(solution)/shard_map/reduce_scatter | solution.py:306
  248.8 3.3 copy-start.2
  252.1 27.3 %copy-start.31 = (bf16[1024,2048]{1,0:T(8,128)(2,1)S(1)}, bf16[1024,2048]{1,0:T(8,128)(2,1)}, u32[]{:S(2)}) copy-start(bf16[1024,2048]{1,0:T(8,128)(2,1)} %all-gather.3.cloned.1.call-done) | copy-start | bytes 12582916
  279.4 3.7 copy-start.15
  279.4 10.0 %slice-start = ((s8[8388608]{0:T(1024)(128)(4,1)}), s8[4194304]{0:T(1024)(128)(4,1)S(1)}, s32[]{:S(2)}) async-start(s8[8388608]{0:T(1024)(128)(4,1)} %bitcast.171), calls=%async_computation.6 | async-start | bytes 8388608
  281.3 8.1 %copy-start.17 = (f32[512,2048]{1,0:T(8,128)S(1)}, f32[512,2048]{1,0:T(8,128)}, u32[]{:S(2)}) copy-start(f32[512,2048]{1,0:T(8,128)} %copy-done.16) | copy-start | bytes 12582916
  281.3 8.1 %slice-start.1 = ((s8[8388608]{0:T(1024)(128)(4,1)}), s8[4194304]{0:T(1024)(128)(4,1)S(1)}, s32[]{:S(2)}) async-start(s8[8388608]{0:T(1024)(128)(4,1)} %bitcast.171), calls=%async_computation.7 | async-start | bytes 8388608
  281.3 26.2 %collective-permute-start.15 = (bf16[1,512,1024]{2,1,0:T(8,128)(2,1)S(1)}, bf16[1,512,1024]{2,1,0:T(8,128)(2,1)S(1)}, u32[]{:S(2)}, u32[]{:S(2)}) collective-permute-start(bf16[1,512,1024]{2,1,0:T(8,128)(2,1)S(1)} %fusion.116), channel_id=1, source_target_pairs={{0,1},{1,0},{2,3},{3,2},{4,5},{5,4},{6,7},{7,6},{8,9},{9,8},{10,11... | collective-permute-start | bytes 3145736 | tf_op jit(solution)/shard_map/ppermute | solution.py:168
  288.8 18.7 %copy-start.32 = (bf16[1024,2048]{1,0:T(8,128)(2,1)S(1)}, bf16[1024,2048]{1,0:T(8,128)(2,1)}, u32[]{:S(2)}) copy-start(bf16[1024,2048]{1,0:T(8,128)(2,1)} %all-gather.3.cloned.1.call-done) | copy-start | bytes 12582916
  288.8 35.6 %collective-permute-start.12 = (bf16[1,512,1024]{2,1,0:T(8,128)(2,1)S(1)}, bf16[1,512,1024]{2,1,0:T(8,128)(2,1)S(1)}, u32[]{:S(2)}, u32[]{:S(2)}) collective-permute-start(bf16[1,512,1024]{2,1,0:T(8,128)(2,1)S(1)} %fusion.104), channel_id=1, source_target_pairs={{0,1},{1,0},{2,3},{3,2},{4,5},{5,4},{6,7},{7,6},{8,9},{9,8},{10,11... | collective-permute-start | bytes 3145736 | tf_op jit(solution)/shard_map/ppermute | solution.py:168
  307.5 16.9 %copy-start.8 = (f32[1,512,1024]{2,1,0:T(8,128)S(1)}, f32[1,512,1024]{2,1,0:T(8,128)}, u32[]{:S(2)}) copy-start(f32[1,512,1024]{2,1,0:T(8,128)} %copy-done.7) | copy-start | bytes 6291460
  307.5 16.9 %copy-start.19 = (bf16[1,512,1024]{2,1,0:T(8,128)(2,1)S(1)}, bf16[1,512,1024]{2,1,0:T(8,128)(2,1)}, u32[]{:S(2)}) copy-start(bf16[1,512,1024]{2,1,0:T(8,128)(2,1)} %copy-done.18) | copy-start | bytes 3145732
  307.5 16.9 %copy-start.20 = (bf16[1,512,1024]{2,1,0:T(8,128)(2,1)S(1)}, bf16[1,512,1024]{2,1,0:T(8,128)(2,1)}, u32[]{:S(2)}) copy-start(bf16[1,512,1024]{2,1,0:T(8,128)(2,1)} %get-tuple-element.87) | copy-start | bytes 3145732
  309.7 14.7 %copy-start.5 = (f32[1,512,1024]{2,1,0:T(8,128)S(1)}, f32[1,512,1024]{2,1,0:T(8,128)}, u32[]{:S(2)}) copy-start(f32[1,512,1024]{2,1,0:T(8,128)} %copy-done.3) | copy-start | bytes 6291460
  309.7 14.7 %copy-start.12 = (bf16[512,1,1024]{2,0,1:T(8,128)(2,1)S(1)}, bf16[512,1,1024]{2,0,1:T(8,128)(2,1)}, u32[]{:S(2)}) copy-start(bf16[512,1,1024]{2,0,1:T(8,128)(2,1)} %param.17) | copy-start | bytes 3145732
  324.4 5.3 %copy-start.27 = (bf16[1,512,1024]{2,1,0:T(8,128)(2,1)S(1)}, bf16[1,512,1024]{2,1,0:T(8,128)(2,1)}, u32[]{:S(2)}) copy-start(bf16[1,512,1024]{2,1,0:T(8,128)(2,1)} %copy-done.26) | copy-start | bytes 3145732
  324.4 5.3 %copy-start.28 = (bf16[1,512,1024]{2,1,0:T(8,128)(2,1)S(1)}, bf16[1,512,1024]{2,1,0:T(8,128)(2,1)}, u32[]{:S(2)}) copy-start(bf16[1,512,1024]{2,1,0:T(8,128)(2,1)} %get-tuple-element.78) | copy-start | bytes 3145732
  327.9 5.9 %copy-start.21 = (bf16[1,1024,1024]{2,1,0:T(8,128)(2,1)S(1)}, bf16[1,1024,1024]{2,1,0:T(8,128)(2,1)}, u32[]{:S(2)}) copy-start(bf16[1,1024,1024]{2,1,0:T(8,128)(2,1)} %pad_maximum_fusion.2) | copy-start | bytes 6291460
  327.9 5.8 %collective-permute-start.16 = (f32[1,6144]{1,0:T(1,128)S(1)}, f32[1,6144]{1,0:T(1,128)S(1)}, u32[]{:S(2)}, u32[]{:S(2)}) collective-permute-start(f32[1,6144]{1,0:T(1,128)S(1)} %constant_dynamic-update-slice_fusion), channel_id=1, source_target_pairs={{0,1},{1,0},{2,3},{3,2},{4,5},{5,4},{6,7},{7,6},{8,9},{9,8},{10,11... | collective-permute-start | bytes 73736 | tf_op jit(solution)/shard_map/ppermute | solution.py:168
  333.7 1.4 collective-permute-start.17
  335.2 4.5 %collective-permute-start.18 = (bf16[2,6144]{1,0:T(2,128)(2,1)S(1)}, bf16[2,6144]{1,0:T(2,128)(2,1)S(1)}, u32[]{:S(2)}, u32[]{:S(2)}) collective-permute-start(bf16[2,6144]{1,0:T(2,128)(2,1)S(1)} %pad_maximum_fusion.10), channel_id=1, source_target_pairs={{0,4},{2,6},{4,0},{6,2},{8,12},{10,14},{12,8},{14,10},{16,20},{18,... | collective-permute-start | bytes 73736 | tf_op jit(solution)/shard_map/ppermute | solution.py:142
  354.7 4.2 collective-permute-start.19
  359.0 21.8 %copy-start.13 = (f32[512,1,1024]{2,0,1:T(8,128)S(1)}, f32[512,1,1024]{2,0,1:T(8,128)}, u32[]{:S(2)}) copy-start(f32[512,1,1024]{2,0,1:T(8,128)} %get-tuple-element.55) | copy-start | bytes 6291460
  359.1 5.6 %collective-permute-start.20 = (bf16[8,6144]{1,0:T(8,128)(2,1)S(1)}, bf16[8,6144]{1,0:T(8,128)(2,1)S(1)}, u32[]{:S(2)}, u32[]{:S(2)}) collective-permute-start(bf16[8,6144]{1,0:T(8,128)(2,1)S(1)} %pad_maximum_fusion.8), channel_id=1, source_target_pairs={{0,16},{2,18},{4,20},{6,22},{8,24},{10,26},{12,28},{14,30},{16,0},... | collective-permute-start | bytes 294920 | tf_op jit(solution)/shard_map/ppermute | solution.py:142
  365.3 4.9 %collective-permute-start.21 = (f32[8,1024]{1,0:T(8,128)S(1)}, f32[8,1024]{1,0:T(8,128)S(1)}, u32[]{:S(2)}, u32[]{:S(2)}) collective-permute-start(f32[8,1024]{1,0:T(8,128)S(1)} %slice_select_fusion.2), channel_id=1, source_target_pairs={{0,16},{2,18},{4,20},{6,22},{8,24},{10,26},{12,28},{14,30},{16,0},... | collective-permute-start | bytes 98312 | tf_op jit(solution)/shard_map/ppermute | solution.py:142
  370.2 3.8 collective-permute-start.22
  374.1 10.2 %collective-permute-start.23 = (f32[2,1024]{1,0:T(2,128)S(1)}, f32[2,1024]{1,0:T(2,128)S(1)}, u32[]{:S(2)}, u32[]{:S(2)}) collective-permute-start(f32[2,1024]{1,0:T(2,128)S(1)} %broadcast_select_fusion.17), channel_id=1, source_target_pairs={{0,4},{2,6},{4,0},{6,2},{8,12},{10,14},{12,8},{14,10},{16,20},{18,... | collective-permute-start | bytes 24584 | tf_op jit(solution)/shard_map/ppermute | solution.py:142
  380.7 3.6 copy-start.34
  380.7 3.6 copy-start.36
  380.8 5.8 %copy-start.37 = (bf16[1,1024]{1,0:T(2,128)(2,1)S(1)}, bf16[1,1024]{1,0:T(2,128)(2,1)}, u32[]{:S(2)}) copy-start(bf16[1,1024]{1,0:T(2,128)(2,1)} %param.10) | copy-start | bytes 6148
  380.8 5.8 %copy-start.38 = (f32[1,1024]{1,0:T(1,128)S(1)}, f32[1,1024]{1,0:T(1,128)}, u32[]{:S(2)}) copy-start(f32[1,1024]{1,0:T(1,128)} %get-tuple-element.53) | copy-start | bytes 12292
  380.8 6.5 %copy-start.29 = (bf16[64,4096]{1,0:T(8,128)(2,1)S(1)}, bf16[64,4096]{1,0:T(8,128)(2,1)}, u32[]{:S(2)}) copy-start(bf16[64,4096]{1,0:T(8,128)(2,1)} %reduce-scatter.3.cloned.1.call-done) | copy-start | bytes 1572868
  384.3 2.3 collective-permute-start.24
  (7 other events, 11.6 us)
Sparse Core Ops, SparseCore 0:
  10.8 59.4 all-gather.2
  73.0 73.9 all-gather.4
  248.9 105.7 reduce-scatter.2
  358.4 72.0 reduce-scatter.4

commit v3 on v2

--- a/solution.py
+++ b/solution.py
@@ -152,15 +152,35 @@
     return value
 
 
-def scatter_small(value):
-    me, bit = lax.axis_index("dp"), lax.axis_size("dp") // 2
+def scatter_step(value, bit):
+    half = value.shape[0] // 2
+    upper = (lax.axis_index("dp") & bit) != 0
+    low_half, high_half = value[:half], value[half:]
+    kept = jnp.where(upper, high_half, low_half)
+    return kept + dp_partner(jnp.where(upper, low_half, high_half), bit)
+
+
+def scatter_small(value, bit):
     while bit >= 1:
-        half = value.shape[0] // 2
+        value = scatter_step(value, bit)
+        bit //= 2
+    return value
+
+
+def scatter_matrix(value, bit_order):
+    me, size, columns = lax.axis_index("dp"), lax.axis_size("dp"), value.shape[1]
+    rows = value.shape[0] // size
+    left = list(range(size.bit_length() - 2, -1, -1))
+    value = value.reshape((2,) * len(left) + (rows, columns))
+    for place in bit_order:
+        axis, bit = left.index(place), 1 << place
         upper = (me & bit) != 0
-        low_half, high_half = value[:half], value[half:]
+        low_half = lax.index_in_dim(value, 0, axis, keepdims=False)
+        high_half = lax.index_in_dim(value, 1, axis, keepdims=False)
+        arrived = dp_partner(jnp.where(upper, low_half, high_half), bit)
         kept = jnp.where(upper, high_half, low_half)
-        value = kept + dp_partner(jnp.where(upper, low_half, high_half), bit)
-        bit //= 2
+        value = (kept.astype(jnp.float32) + arrived.astype(jnp.float32)).astype(jnp.bfloat16)
+        left.pop(axis)
     return value
 
 
@@ -211,10 +231,9 @@
     own_cotangent = cotangent.transpose(1, 0, 2)
     token_parts = spread(own_tokens)
     cotangent_parts = spread(own_cotangent)
-    token_parts, cotangent_parts = lax.optimization_barrier((token_parts, cotangent_parts))
     cond_value = cond.astype(jnp.float32)
     cond_act = jax.nn.silu(cond_value).astype(jnp.bfloat16)
-    all_cond_act = gather_small(cond_act)
+    all_cond_act, token_parts = lax.optimization_barrier((gather_small(cond_act), token_parts))
     ada_rows, ada_columns = ada_weight.shape
     bias_columns = ada_bias.shape[0]
     my_cond_act = lax.dynamic_slice_in_dim(all_cond_act, me * ada_rows, ada_rows, axis=1)
@@ -225,7 +244,10 @@
         me * bias_columns,
         axis=0,
     )
-    modulation = scatter_small(mod_term + placed_bias[None, :])
+    mod_term, cotangent_parts = lax.optimization_barrier(
+        (scatter_step(mod_term + placed_bias[None, :], lax.axis_size("dp") // 2), cotangent_parts)
+    )
+    modulation = scatter_small(mod_term, lax.axis_size("dp") // 4)
     shift1, scale1, gate1, shift2, scale2, gate2 = jnp.split(modulation[:, None, :], 6, axis=-1)
     residual = own_tokens.astype(jnp.float32)
     full_normed1 = joined(
@@ -264,7 +286,6 @@
         grad_inner_parts.append(
             jax.vjp(gelu_tanh, inner_part)[1](grad_act)[0].astype(jnp.bfloat16)
         )
-    grad_normed2 = collect(grad_inner_parts, w_up)
     grad_down = jnp.einsum(
         "lsf,lse->fe",
         joined(grad_mlp_parts),
@@ -280,14 +301,15 @@
     second_grads = jnp.concatenate(
         [grad_up.astype(jnp.bfloat16), grad_down.astype(jnp.bfloat16)], axis=1
     )
+    grad_inner_parts, second_grads = lax.optimization_barrier((grad_inner_parts, second_grads))
+    second_grads = lax.psum_scatter(second_grads, "dp", scatter_dimension=0, tiled=True)
+    grad_normed2 = collect(grad_inner_parts, w_up)
     mod_pull2 = jax.vjp(modulate, middle, shift2, scale2)[1]
     grad_middle, grad_shift2, grad_scale2 = mod_pull2(grad_normed2)
     grad_middle = grad_middle + grad_output
     grad_gate1 = jnp.sum(grad_middle * branch, axis=1)
     grad_branch = (grad_middle * gate1).astype(jnp.bfloat16)
     full_grad_branch = joined(spread(grad_branch))
-    full_grad_branch, second_grads = lax.optimization_barrier((full_grad_branch, second_grads))
-    second_grads = lax.psum_scatter(second_grads, "dp", scatter_dimension=0, tiled=True)
     grad_attended = jnp.einsum(
         "lsf,fe->lse", full_grad_branch, w_out, preferred_element_type=jnp.float32
     ).astype(jnp.bfloat16)
@@ -300,10 +322,17 @@
     grad_qkv = jnp.einsum(
         "lsd,lsw->dw", full_normed1, grad_query_key_value, preferred_element_type=jnp.float32
     ).astype(jnp.bfloat16)
-    first_grads, second_grads = lax.optimization_barrier(
-        (jnp.concatenate([grad_qkv, grad_out], axis=1), second_grads)
-    )
-    first_grads = lax.psum_scatter(first_grads, "dp", scatter_dimension=0, tiled=True)
+    places = list(range(lax.axis_size("dp").bit_length() - 1))
+    orders = (places, places[:1] + places[2:] + places[1:2])
+    half_columns = qkv_columns // 2
+    grad_out = scatter_matrix(grad_out, orders[0])
+    grad_qkv = jnp.concatenate(
+        [
+            scatter_matrix(grad_qkv[:, :half_columns], orders[0]),
+            scatter_matrix(grad_qkv[:, half_columns:], orders[1]),
+        ],
+        axis=1,
+    )
     grad_parts = (
         [grad_query_key_value[:, :own_count], grad_query_key_value[:, own_count:]]
         if len(token_parts) == 2
@@ -344,7 +373,8 @@
     grad_cond_act = scatter_small(
         lax.dynamic_update_slice_in_dim(
             jnp.zeros((cond_term.shape[0], width), jnp.float32), cond_term, me * ada_rows, axis=1
-        )
+        ),
+        lax.axis_size("dp") // 2,
     )
     sigmoid_c = jax.nn.sigmoid(cond_value)
     grad_cond = grad_cond_act * sigmoid_c * (1.0 + cond_value * (1.0 - sigmoid_c))
@@ -352,8 +382,8 @@
         mixed.transpose(1, 0, 2),
         grad_tokens.transpose(1, 0, 2),
         grad_cond,
-        first_grads[:, :qkv_columns].astype(jnp.float32),
-        first_grads[:, qkv_columns:].astype(jnp.float32),
+        grad_qkv.astype(jnp.float32),
+        grad_out.astype(jnp.float32),
         second_grads[:, :up_columns].astype(jnp.float32),
         second_grads[:, up_columns:].astype(jnp.float32),
         grad_ada,

time: 446 us -> 424 us (0.951)
  waiting for transfers between devices: 218 us -> 177 us
  matrix products: 68.8 us -> 89.4 us
  other arithmetic: 42.8 us -> 38 us
    ppermute x16 -> x28, waiting for transfers between devices: 35 us -> 77.7 us  [dp_partner(): lax.ppermute(value, 'dp', [(index, index ^ bit) for index in range(size)])]
    reduce_scatter x1 -> x0, waiting for transfers between devices: 42.2 us -> none  [body(): lax.psum_scatter(first_grads, 'dp', scatter_dimension=0, tiled=True)]
    ppermute x9, waiting for transfers between devices: 126 us -> 98.8 us  [swap(): return lax.ppermute(value, 'tensor', [(0, 1), (1, 0)])]
    reduce_scatter x1, waiting for transfers between devices: 14.8 us -> 0.01 us  [body(): lax.psum_scatter(second_grads, 'dp', scatter_dimension=0, tiled=True)]
    dot_general x2, matrix products: 9.96 us -> 22 us  [body(): jnp.einsum('lsf,fe->lse', grad_part, w_down, preferred_element_type=jnp.f...]
    dot_general x8, matrix products: 20.5 us -> 27.2 us  [term(): jnp.einsum('lse,fe->lsf', part, weight, preferred_element_type=jnp.float32)]
    concatenate x2 -> x0, other arithmetic: 5.65 us -> none  [the longest x1 3.02 us: joined(): return parts[0] if len(parts) == 1 else jnp.concatenate(parts, axis=1)]
    ppermute x16 -> x28, starting transfers between devices: 24.9 us -> 27.6 us  [dp_partner(): lax.ppermute(value, 'dp', [(index, index ^ bit) for index in range(size)])]
  transfers between devices with their start and end apart: 29 -> 40, of which waited for: 22 -> 24; matrix products, arithmetic and copies ran while one was open for 21% -> 16% of each run, Pallas kernels for 10% -> 11%
where the time goes in v3:
time: 424 us; the launch traced here: 416 us
  waiting for transfers between devices  177 us (42%)
  matrix products  89.4 us (21%)
  Pallas kernels  44.6 us (11%)
  other arithmetic  38 us (9%)
  starting transfers between devices  37.2 us (9%)
  local copies, waits for them, and re-layouts  15.2 us (4%)
  between operations  15 us (4%)
    ppermute x9, waiting for transfers between devices, swap(): return lax.ppermute(value, 'tensor', [(0, 1), (1, 0)])  98.8 us
    ppermute x28, waiting for transfers between devices, dp_partner(): lax.ppermute(value, 'dp', [(index, index ^ bit) for index in range(size)])  77.7 us
    ppermute x28, starting transfers between devices, dp_partner(): lax.ppermute(value, 'dp', [(index, index ^ bit) for index in range(size)])  27.6 us
    dot_general x8, matrix products, term(): jnp.einsum('lse,fe->lsf', part, weight, preferred_element_type=jnp.float32)  27.2 us
    pallas_call x1, Pallas kernels, attention_backward(): pl.pallas_call(functools.partial(backward_kernel, score_scale), grid=(lat...  27.1 us
    dot_general x2, matrix products, body(): jnp.einsum('lsf,fe->lse', grad_part, w_down, preferred_element_type=jnp.f...  22 us
    pallas_call x1, Pallas kernels, attention_forward(): pl.pallas_call(functools.partial(forward_kernel, score_scale), grid=(late...  17.5 us
    unnamed x85, local copies, waits for them, and re-layouts  14.4 us
  transfers between devices with their start and end apart: 40, of which 24 were waited for; matrix products, arithmetic and copies ran while one was open for 16% of the time, Pallas kernels for 11%

profile of v3, /device:TPU:0, one launch (start us, length us, event | category | flops | bytes accessed | tf_op | source)
XLA Modules:
  0.0 416.0 jit_solution(14145941017278454999)
XLA Ops:
  7.2 1.8 pad_maximum_fusion.2
  11.7 2.9 collective-permute-start.1
  14.6 1.5 collective-permute-start.4
  16.7 1.7 collective-permute-start.2
  18.4 1.9 pad_maximum_fusion.1
  20.5 2.7 collective-permute-start.3
  25.3 15.6 %collective-permute-done.4 = bf16[1,512,1024]{2,1,0:T(8,128)(2,1)S(1)} collective-permute-done((bf16[1,512,1024]{2,1,0:T(8,128)(2,1)}, bf16[1,512,1024]{2,1,0:T(8,128)(2,1)S(1)}, u32[]{:S(2)}, u32[]{:S(2)}) %collective-permute-start.4) | collective-permute-done | bytes 1048608 | tf_op jit(solution)/shard_map/ppermute | solution.py:188
  41.2 2.7 collective-permute-start.5
  44.7 18.4 %collective-permute-done.5 = f32[8,6144]{1,0:T(8,128)S(1)} collective-permute-done((f32[8,6144]{1,0:T(8,128)S(1)}, f32[8,6144]{1,0:T(8,128)S(1)}, u32[]{:S(2)}, u32[]{:S(2)}) %collective-permute-start.5) | collective-permute-done | bytes 196640 | tf_op jit(solution)/shard_map/ppermute | solution.py:142
  64.1 5.2 %collective-permute-done.7 = f32[4,6144]{1,0:T(4,128)S(1)} collective-permute-done((f32[4,6144]{1,0:T(4,128)S(1)}, f32[4,6144]{1,0:T(4,128)S(1)}, u32[]{:S(2)}, u32[]{:S(2)}) %collective-permute-start.7) | collective-permute-done | bytes 98336 | tf_op jit(solution)/shard_map/ppermute | solution.py:142
  70.0 3.5 collective-permute-done.8
  75.5 2.1 fusion.60
  77.7 6.2 %fusion.22.qkv_ref = bf16[1,1024,1536]{2,1,0:T(8,128)(2,1)S(1)} fusion(bf16[1024,2048]{1,0:T(8,128)(2,1)} %all-gather.3.cloned.1.call-done, bf16[1,512,1024]{2,1,0:T(8,128)(2,1)} %get-tuple-element.88, bf16[1,512,1024]{2,1,0:T(8,128)(2,1)} %get-tuple-element.87), kind=kOutput, calls=%fused_computation.34 | convolution fusion | flops 3226992640 | bytes 8388608 | tf_op jit(solution)/shard_map/lsd,dw->lsw/dot_general | solution.py:259
  83.9 17.5 %attention_forward.1 = (bf16[1,1024,512]{2,1,0:T(8,128)(2,1)S(1)}, f32[1,4,2,1024]{3,2,1,0:T(2,128)S(1)}) custom-call(bf16[1,1024,1536]{2,1,0:T(8,128)(2,1)S(1)} %fusion.22.qkv_ref), custom_call_target="tpu_custom_call" | custom-call | flops 8589934592 | bytes 4194304 | tf_op jit(solution)/shard_map/attention_forward/pallas_call | solution.py:101
  103.4 24.0 %collective-permute-done.10 = bf16[1,512,1024]{2,1,0:T(8,128)(2,1)S(1)} collective-permute-done((bf16[1,512,1024]{2,1,0:T(8,128)(2,1)S(1)}, bf16[1,512,1024]{2,1,0:T(8,128)(2,1)S(1)}, u32[]{:S(2)}, u32[]{:S(2)}) %collective-permute-start.10) | collective-permute-done | bytes 1048608 | tf_op jit(solution)/shard_map/ppermute | solution.py:188
  128.4 2.0 fusion.180
  132.5 3.1 multiply_convert_fusion.3
  135.6 20.2 %collective-permute-done.11 = bf16[1,512,1024]{2,1,0:T(8,128)(2,1)} collective-permute-done((bf16[1,512,1024]{2,1,0:T(8,128)(2,1)S(1)}, bf16[1,512,1024]{2,1,0:T(8,128)(2,1)}, u32[]{:S(2)}, u32[]{:S(2)}) %collective-permute-start.11) | collective-permute-done | bytes 1048608 | tf_op jit(solution)/shard_map/ppermute | solution.py:188
  155.8 5.0 %fusion.40 = f32[512,2048]{1,0:T(8,128)S(1)} fusion(bf16[1024,4096]{1,0:T(8,128)(2,1)} %all-gather.5.cloned.1.call-done, bf16[1,512,1024]{2,1,0:T(8,128)(2,1)} %collective-permute-done.11), kind=kOutput, calls=%fused_computation.57 | convolution fusion | flops 2147483648 | bytes 9437184 | tf_op jit(solution)/shard_map/lsd,dw->lsw/dot_general | solution.py:272
  162.8 2.4 fusion.42
  168.3 6.3 %fusion.20 = bf16[1024,2048]{1,0:T(8,128)(2,1)} fusion(bf16[1,512,2048]{2,1,0:T(8,128)(2,1)S(1)} %fusion.178, bf16[1,512,2048]{2,1,0:T(8,128)(2,1)S(1)} %fusion.177, bf16[1,512,1024]{2,1,0:T(8,128)(2,1)S(1)} %copy-done.20, bf16[1,512,1024]{2,1,0:T(8,128)(2,1)S(1)} %copy-done.21), kind=kOutput, calls=%fused_computation.30 | convolution fusion | flops 4309647360 | bytes 10485760 | tf_op jit(solution)/shard_map/lsf,lse->fe/dot_general | solution.py:289
  174.6 17.3 %fusion.73 = bf16[1,512,2048]{2,1,0:T(8,128)(2,1)S(1)} fusion(f32[512,2048]{1,0:T(8,128)S(1)} %fusion.42, bf16[1024,4096]{1,0:T(8,128)(2,1)S(1)} %copy-done.33, bf16[1,512,1024]{2,1,0:T(8,128)(2,1)S(1)} %copy-done.21), kind=kOutput, calls=%fused_computation.114 | convolution fusion | flops 2168455168 | bytes 11534336 | tf_op jit(solution)/shard_map/lsf,fe->lse/dot_general | solution.py:285
  191.9 4.7 %fusion.72 = bf16[1,512,2048]{2,1,0:T(8,128)(2,1)S(1)} fusion(f32[512,2048]{1,0:T(8,128)S(1)} %fusion.40, bf16[1024,4096]{1,0:T(8,128)(2,1)S(1)} %copy-done.33, bf16[1,512,1024]{2,1,0:T(8,128)(2,1)S(1)} %copy-done.20), kind=kOutput, calls=%fused_computation.113 | convolution fusion | flops 2168455168 | bytes 11534336 | tf_op jit(solution)/shard_map/lsf,fe->lse/dot_general | solution.py:285
  196.6 1.3 copy-done.34
  197.9 7.5 %fusion.21 = bf16[1024,2048]{1,0:T(8,128)(2,1)} fusion(bf16[1,512,2048]{2,1,0:T(8,128)(2,1)S(1)} %fusion.72, bf16[1,512,2048]{2,1,0:T(8,128)(2,1)S(1)} %fusion.73, bf16[1,512,1024]{2,1,0:T(8,128)(2,1)} %collective-permute-done.11, bf16[1,512,1024]{2,1,0:T(8,128)(2,1)S(1)} %copy-done.23), kind=kOutput, calls=%fused_computation.31 | convolution fusion | flops 4309647360 | bytes 10485760 | tf_op jit(solution)/shard_map/lsd,lse->de/dot_general | solution.py:295
  205.4 7.8 %pad_maximum_fusion = bf16[1024,4096]{1,0:T(8,128)(2,1)} fusion(bf16[1024,2048]{1,0:T(8,128)(2,1)} %fusion.20, bf16[1024,2048]{1,0:T(8,128)(2,1)} %fusion.21), kind=kLoop, calls=%fused_computation | loop fusion | flops 16777216 | bytes 16777216 | tf_op jit(solution)/shard_map/concatenate | solution.py:301
  213.2 5.3 %fusion.110 = bf16[1,512,1024]{2,1,0:T(8,128)(2,1)S(1)} fusion(bf16[1024,4096]{1,0:T(8,128)(2,1)} %all-gather.5.cloned.1.call-done, bf16[1,512,2048]{2,1,0:T(8,128)(2,1)} %copy-done.34), kind=kOutput, calls=%fused_computation.135 | convolution fusion | flops 2148007936 | bytes 7340032 | tf_op jit(solution)/shard_map/lse,fe->lsf/dot_general | solution.py:203
  218.5 1.3 collective-permute-start.13
  219.9 22.3 %collective-permute-done.13 = bf16[1,512,1024]{2,1,0:T(8,128)(2,1)S(1)} collective-permute-done((bf16[1,512,1024]{2,1,0:T(8,128)(2,1)S(1)}, bf16[1,512,1024]{2,1,0:T(8,128)(2,1)S(1)}, u32[]{:S(2)}, u32[]{:S(2)}) %collective-permute-start.13) | collective-permute-done | bytes 1048608 | tf_op jit(solution)/shard_map/ppermute | solution.py:188
  242.1 5.3 %multiply_reduce_fusion = (f32[1024]{0:T(1024)S(1)}, f32[512]{0:T(512)S(1)}, f32[1024]{0:T(1024)S(1)}, bf16[1,512,1024]{2,1,0:T(8,128)(2,1)S(1)}) fusion(bf16[1,512,1024]{2,1,0:T(8,128)(2,1)S(1)} %collective-permute-done.13, f32[1,512,1024]{2,1,0:T(8,128)S(1)} %copy-done.4, f32[512]{0:T(512)S(1)} %fusion.164, f32[512]{0:T(512)S(1)} %broadcast_multiply_fusion.1, ...), kind=kOutput, calls=%fused_computation.103 | convolution fusion | flops 2153772544 | bytes 10504192 | tf_op jit(solution)/shard_map/lse,fe->lsf/dot_general | solution.py:203
  249.6 1.4 multiply_convert_fusion.2
  251.0 1.3 collective-permute-start.14
  252.3 3.7 fusion.104
  256.8 6.3 %fusion.107 = bf16[1,512,1024]{2,1,0:T(8,128)(2,1)S(1)} fusion(bf16[1024,4096]{1,0:T(8,128)(2,1)} %all-gather.5.cloned.1.call-done, f32[512,2048]{1,0:T(8,128)} %copy-done.14), kind=kOutput, calls=%fused_computation.134 | convolution fusion | flops 2157445120 | bytes 9437184 | tf_op jit(solution)/shard_map/lse,fe->lsf/dot_general | solution.py:203
  263.1 14.4 %collective-permute-done.14 = bf16[1,512,1024]{2,1,0:T(8,128)(2,1)} collective-permute-done((bf16[1,512,1024]{2,1,0:T(8,128)(2,1)}, bf16[1,512,1024]{2,1,0:T(8,128)(2,1)}, u32[]{:S(2)}, u32[]{:S(2)}) %collective-permute-start.14) | collective-permute-done | bytes 1048608 | tf_op jit(solution)/shard_map/ppermute | solution.py:188
  277.4 3.1 fusion.120.grad_ref
  280.6 27.1 %attention_backward.1 = bf16[1,1024,1536]{2,1,0:T(8,128)(2,1)S(1)} custom-call(bf16[1,1024,1536]{2,1,0:T(8,128)(2,1)S(1)} %copy-done.2, bf16[1,1024,512]{2,1,0:T(8,128)(2,1)S(1)} %fusion.120.grad_ref, f32[1,4,2,1024]{3,2,1,0:T(2,128)S(1)} %get-tuple-element.29.log_ref), custom_call_target="tpu_custom_call" | custom-call | flops 21474836480 | bytes 7340032 | tf_op jit(solution)/shard_map/attention_backward/pallas_call | solution.py:122
  307.7 4.1 convolution_convert_fusion
  311.8 1.8 fusion.121
  313.6 1.4 collective-permute-start.15
  315.6 2.8 convolution_convert_fusion.2
  321.5 1.7 collective-permute-start.30
  323.7 1.7 collective-permute-start.26
  325.4 10.5 %collective-permute-done.34 = bf16[2,2,64,512]{3,2,0,1:T(8,128)(2,1)S(1)} collective-permute-done((bf16[2,2,64,512]{3,2,0,1:T(8,128)(2,1)S(1)}, bf16[2,2,64,512]{3,2,0,1:T(8,128)(2,1)S(1)}, u32[]{:S(2)}, u32[]{:S(2)}) %collective-permute-start.34) | collective-permute-done | bytes 262176 | tf_op jit(solution)/shard_map/ppermute | solution.py:142
  336.0 2.1 fusion.62
  340.1 3.4 fusion.61
  343.8 1.4 collective-permute-start.35
  345.2 2.4 collective-permute-done.16
  349.5 2.0 collective-permute-start.36
  351.5 1.9 collective-permute-done.18
  354.8 3.9 collective-permute-done.36
  359.4 3.5 copy.28
  362.9 3.5 copy.29
  366.8 8.9 %collective-permute-done.20 = bf16[8,6144]{1,0:T(8,128)(2,1)S(1)} collective-permute-done((bf16[8,6144]{1,0:T(8,128)(2,1)S(1)}, bf16[8,6144]{1,0:T(8,128)(2,1)S(1)}, u32[]{:S(2)}, u32[]{:S(2)}) %collective-permute-start.20) | collective-permute-done | bytes 98336 | tf_op jit(solution)/shard_map/ppermute | solution.py:142
  376.5 3.0 collective-permute-start.31
  379.5 6.3 %collective-permute-done.21 = f32[8,1024]{1,0:T(8,128)S(1)} collective-permute-done((f32[8,1024]{1,0:T(8,128)S(1)}, f32[8,1024]{1,0:T(8,128)S(1)}, u32[]{:S(2)}, u32[]{:S(2)}) %collective-permute-start.21) | collective-permute-done | bytes 32800 | tf_op jit(solution)/shard_map/ppermute | solution.py:142
  386.1 3.8 collective-permute-done.22
  390.0 1.5 collective-permute-start.23
  391.6 2.1 collective-permute-done.23
  393.8 2.3 fusion.153
  397.4 1.5 collective-permute-start.32
  399.1 3.5 collective-permute-done.32
  402.7 3.7 collective-permute-done.28
  407.2 2.1 slice_convert_fusion
  (225 shorter events, 37.4 us)
Async XLA Ops:
  7.2 33.7 %copy-start = (bf16[64,6144]{1,0:T(8,128)(2,1)S(1)}, bf16[64,6144]{1,0:T(8,128)(2,1)}, u32[]{:S(2)}) copy-start(bf16[64,6144]{1,0:T(8,128)(2,1)} %param.15) | copy-start | bytes 2359300
  7.2 36.7 %copy-start.6 = (bf16[512,1,1024]{2,0,1:T(8,128)(2,1)S(1)}, bf16[512,1,1024]{2,0,1:T(8,128)(2,1)}, u32[]{:S(2)}) copy-start(bf16[512,1,1024]{2,0,1:T(8,128)(2,1)} %param.9) | copy-start | bytes 3145732
  7.2 70.5 %all-gather.3.cloned.1.call-start = ((), (), s32[]{:S(2)}) async-start(), calls=%async_computation.1 | async-start | bytes 4456448 | tf_op jit(solution)/shard_map/all_gather | solution.py:222
  9.1 146.7 %all-gather.5.cloned.1.call-start = ((), (), s32[]{:S(2)}) async-start(), calls=%async_computation.2 | async-start | bytes 8912896 | tf_op jit(solution)/shard_map/all_gather | solution.py:225
  10.4 1.3 collective-permute-start
  11.7 4.9 %collective-permute-start.1 = (bf16[2,1024]{1,0:T(2,128)(2,1)S(1)}, bf16[2,1024]{1,0:T(2,128)(2,1)S(1)}, u32[]{:S(2)}, u32[]{:S(2)}) collective-permute-start(bf16[2,1024]{1,0:T(2,128)(2,1)S(1)} %pad_maximum_fusion.12), channel_id=1, source_target_pairs={{0,4},{2,6},{4,0},{6,2},{8,12},{10,14},{12,8},{14,10},{16,20},{18,... | collective-permute-start | bytes 12296 | tf_op jit(solution)/shard_map/ppermute | solution.py:142
  14.6 26.3 %collective-permute-start.4 = (bf16[1,512,1024]{2,1,0:T(8,128)(2,1)}, bf16[1,512,1024]{2,1,0:T(8,128)(2,1)S(1)}, u32[]{:S(2)}, u32[]{:S(2)}) collective-permute-start(bf16[1,512,1024]{2,1,0:T(8,128)(2,1)} %bitcast.234), channel_id=1, source_target_pairs={{0,1},{1,0},{2,3},{3,2},{4,5},{5,4},{6,7},{7,6},{8,9},{9,8},{10,11... | collective-permute-start | bytes 3145736 | tf_op jit(solution)/shard_map/ppermute | solution.py:188
  16.2 47.0 %collective-permute-start.6 = (bf16[1,512,1024]{2,1,0:T(8,128)(2,1)}, bf16[1,512,1024]{2,1,0:T(8,128)(2,1)}, u32[]{:S(2)}, u32[]{:S(2)}) collective-permute-start(bf16[1,512,1024]{2,1,0:T(8,128)(2,1)} %bitcast.238), channel_id=1, source_target_pairs={{0,1},{1,0},{2,3},{3,2},{4,5},{5,4},{6,7},{7,6},{8,9},{9,8},{10,11... | collective-permute-start | bytes 3145736 | tf_op jit(solution)/shard_map/ppermute | solution.py:188
  16.7 3.7 collective-permute-start.2
  20.3 386.9 %reduce-scatter.2.cloned.1.call-start = ((), (), s32[]{:S(2)}) async-start(), calls=%async_computation.3 | async-start | bytes 8912896 | tf_op jit(solution)/shard_map/reduce_scatter | solution.py:305
  20.5 4.8 %collective-permute-start.3 = (bf16[8,1024]{1,0:T(8,128)(2,1)S(1)}, bf16[8,1024]{1,0:T(8,128)(2,1)S(1)}, u32[]{:S(2)}, u32[]{:S(2)}) collective-permute-start(bf16[8,1024]{1,0:T(8,128)(2,1)S(1)} %pad_maximum_fusion.10), channel_id=1, source_target_pairs={{0,16},{2,18},{4,20},{6,22},{8,24},{10,26},{12,28},{14,30},{16,0},... | collective-permute-start | bytes 49160 | tf_op jit(solution)/shard_map/ppermute | solution.py:142
  25.3 15.9 %copy-start.30 = (bf16[16,1024]{1,0:T(8,128)(2,1)}, bf16[16,1024]{1,0:T(8,128)(2,1)S(1)}, u32[]{:S(2)}) copy-start(bf16[16,1024]{1,0:T(8,128)(2,1)S(1)} %pad_maximum_fusion.8) | copy-start | bytes 98308
  41.2 21.9 %collective-permute-start.5 = (f32[8,6144]{1,0:T(8,128)S(1)}, f32[8,6144]{1,0:T(8,128)S(1)}, u32[]{:S(2)}, u32[]{:S(2)}) collective-permute-start(f32[8,6144]{1,0:T(8,128)S(1)} %slice_select_fusion), channel_id=1, source_target_pairs={{0,16},{2,18},{4,20},{6,22},{8,24},{10,26},{12,28},{14,30},{16,0},... | collective-permute-start | bytes 589832 | tf_op jit(solution)/shard_map/ppermute | solution.py:142
  63.2 6.1 %collective-permute-start.7 = (f32[4,6144]{1,0:T(4,128)S(1)}, f32[4,6144]{1,0:T(4,128)S(1)}, u32[]{:S(2)}, u32[]{:S(2)}) collective-permute-start(f32[4,6144]{1,0:T(4,128)S(1)} %slice_select_fusion.1), channel_id=1, source_target_pairs={{0,8},{2,10},{4,12},{6,14},{8,0},{10,2},{12,4},{14,6},{16,24},{18,... | collective-permute-start | bytes 294920 | tf_op jit(solution)/shard_map/ppermute | solution.py:142
  69.4 4.2 collective-permute-start.8
  73.6 1.3 collective-permute-start.9
  83.9 17.5 %copy-start.1 = (bf16[1,1024,1536]{2,1,0:T(8,128)(2,1)}, bf16[1,1024,1536]{2,1,0:T(8,128)(2,1)S(1)}, u32[]{:S(2)}) copy-start(bf16[1,1024,1536]{2,1,0:T(8,128)(2,1)S(1)} %fusion.22.qkv_ref) | copy-start | bytes 9437188
  83.9 17.5 %copy-start.26 = (bf16[1024,2048]{1,0:T(8,128)(2,1)S(1)}, bf16[1024,2048]{1,0:T(8,128)(2,1)}, u32[]{:S(2)}) copy-start(bf16[1024,2048]{1,0:T(8,128)(2,1)} %all-gather.3.cloned.1.call-done) | copy-start | bytes 12582916
  102.2 25.2 %collective-permute-start.10 = (bf16[1,512,1024]{2,1,0:T(8,128)(2,1)S(1)}, bf16[1,512,1024]{2,1,0:T(8,128)(2,1)S(1)}, u32[]{:S(2)}, u32[]{:S(2)}) collective-permute-start(bf16[1,512,1024]{2,1,0:T(8,128)(2,1)S(1)} %fusion.128), channel_id=1, source_target_pairs={{0,1},{1,0},{2,3},{3,2},{4,5},{5,4},{6,7},{7,6},{8,9},{9,8},{10,11... | collective-permute-start | bytes 3145736 | tf_op jit(solution)/shard_map/ppermute | solution.py:188
  130.4 5.2 %copy-start.3 = (f32[1,512,1024]{2,1,0:T(8,128)}, f32[1,512,1024]{2,1,0:T(8,128)S(1)}, u32[]{:S(2)}) copy-start(f32[1,512,1024]{2,1,0:T(8,128)S(1)} %get-tuple-element.53) | copy-start | bytes 6291460
  131.2 4.4 %copy-start.22 = (bf16[1,512,1024]{2,1,0:T(8,128)(2,1)}, bf16[1,512,1024]{2,1,0:T(8,128)(2,1)S(1)}, u32[]{:S(2)}) copy-start(bf16[1,512,1024]{2,1,0:T(8,128)(2,1)S(1)} %add_convert_fusion) | copy-start | bytes 3145732
  131.2 24.6 %collective-permute-start.11 = (bf16[1,512,1024]{2,1,0:T(8,128)(2,1)S(1)}, bf16[1,512,1024]{2,1,0:T(8,128)(2,1)}, u32[]{:S(2)}, u32[]{:S(2)}) collective-permute-start(bf16[1,512,1024]{2,1,0:T(8,128)(2,1)S(1)} %add_convert_fusion), channel_id=1, source_target_pairs={{0,1},{1,0},{2,3},{3,2},{4,5},{5,4},{6,7},{7,6},{8,9},{9,8},{10,11... | collective-permute-start | bytes 3145736 | tf_op jit(solution)/shard_map/ppermute | solution.py:188
  155.8 6.3 %copy-start.33 = (bf16[1024,4096]{1,0:T(8,128)(2,1)S(1)}, bf16[1024,4096]{1,0:T(8,128)(2,1)}, u32[]{:S(2)}) copy-start(bf16[1024,4096]{1,0:T(8,128)(2,1)} %all-gather.5.cloned.1.call-done) | copy-start | bytes 25165828
  160.8 31.0 %copy-start.15 = (f32[512,2048]{1,0:T(8,128)}, f32[512,2048]{1,0:T(8,128)S(1)}, u32[]{:S(2)}) copy-start(f32[512,2048]{1,0:T(8,128)S(1)} %fusion.40) | copy-start | bytes 12582916
  165.2 9.4 %copy-start.14 = (f32[512,2048]{1,0:T(8,128)}, f32[512,2048]{1,0:T(8,128)S(1)}, u32[]{:S(2)}) copy-start(f32[512,2048]{1,0:T(8,128)S(1)} %fusion.42) | copy-start | bytes 12582916
  191.9 4.7 %copy-start.35 = (bf16[1,512,2048]{2,1,0:T(8,128)(2,1)}, bf16[1,512,2048]{2,1,0:T(8,128)(2,1)S(1)}, u32[]{:S(2)}) copy-start(bf16[1,512,2048]{2,1,0:T(8,128)(2,1)S(1)} %fusion.73) | copy-start | bytes 6291460
  213.2 28.9 %copy-start.4 = (f32[1,512,1024]{2,1,0:T(8,128)S(1)}, f32[1,512,1024]{2,1,0:T(8,128)}, u32[]{:S(2)}) copy-start(f32[1,512,1024]{2,1,0:T(8,128)} %copy-done.3) | copy-start | bytes 6291460
  213.2 28.9 %copy-start.36 = (bf16[1,512,2048]{2,1,0:T(8,128)(2,1)S(1)}, bf16[1,512,2048]{2,1,0:T(8,128)(2,1)}, u32[]{:S(2)}) copy-start(bf16[1,512,2048]{2,1,0:T(8,128)(2,1)} %copy-done.35) | copy-start | bytes 6291460
  213.2 39.1 %slice-start = ((s8[8388608]{0:T(1024)(128)(4,1)}), s8[4194304]{0:T(1024)(128)(4,1)S(1)}, s32[]{:S(2)}) async-start(s8[8388608]{0:T(1024)(128)(4,1)} %bitcast.262), calls=%async_computation.4 | async-start | bytes 8388608
  218.5 23.6 %collective-permute-start.13 = (bf16[1,512,1024]{2,1,0:T(8,128)(2,1)S(1)}, bf16[1,512,1024]{2,1,0:T(8,128)(2,1)S(1)}, u32[]{:S(2)}, u32[]{:S(2)}) collective-permute-start(bf16[1,512,1024]{2,1,0:T(8,128)(2,1)S(1)} %fusion.110), channel_id=1, source_target_pairs={{0,1},{1,0},{2,3},{3,2},{4,5},{5,4},{6,7},{7,6},{8,9},{9,8},{10,11... | collective-permute-start | bytes 3145736 | tf_op jit(solution)/shard_map/ppermute | solution.py:188
  219.9 32.5 %slice-start.1 = ((s8[8388608]{0:T(1024)(128)(4,1)}), s8[4194304]{0:T(1024)(128)(4,1)S(1)}, s32[]{:S(2)}) async-start(s8[8388608]{0:T(1024)(128)(4,1)} %bitcast.262), calls=%async_computation.5 | async-start | bytes 8388608
  251.0 26.4 %collective-permute-start.14 = (bf16[1,512,1024]{2,1,0:T(8,128)(2,1)}, bf16[1,512,1024]{2,1,0:T(8,128)(2,1)}, u32[]{:S(2)}, u32[]{:S(2)}) collective-permute-start(bf16[1,512,1024]{2,1,0:T(8,128)(2,1)} %multiply_convert_fusion.2), channel_id=1, source_target_pairs={{0,1},{1,0},{2,3},{3,2},{4,5},{5,4},{6,7},{7,6},{8,9},{9,8},{10,11... | collective-permute-start | bytes 3145736 | tf_op jit(solution)/shard_map/ppermute | solution.py:188
  256.0 83.4 %collective-permute-start.12 = (bf16[1,512,1024]{2,1,0:T(8,128)(2,1)}, bf16[1,512,1024]{2,1,0:T(8,128)(2,1)}, u32[]{:S(2)}, u32[]{:S(2)}) collective-permute-start(bf16[1,512,1024]{2,1,0:T(8,128)(2,1)} %fusion.104), channel_id=1, source_target_pairs={{0,1},{1,0},{2,3},{3,2},{4,5},{5,4},{6,7},{7,6},{8,9},{9,8},{10,11... | collective-permute-start | bytes 3145736 | tf_op jit(solution)/shard_map/ppermute | solution.py:188
  256.8 20.7 %copy-start.27 = (bf16[1024,2048]{1,0:T(8,128)(2,1)S(1)}, bf16[1024,2048]{1,0:T(8,128)(2,1)}, u32[]{:S(2)}) copy-start(bf16[1024,2048]{1,0:T(8,128)(2,1)} %all-gather.3.cloned.1.call-done) | copy-start | bytes 12582916
  263.1 17.5 %copy-start.2 = (bf16[1,1024,1536]{2,1,0:T(8,128)(2,1)S(1)}, bf16[1,1024,1536]{2,1,0:T(8,128)(2,1)}, u32[]{:S(2)}) copy-start(bf16[1,1024,1536]{2,1,0:T(8,128)(2,1)} %copy-done.1) | copy-start | bytes 9437188
  280.5 27.1 %copy-start.24 = (bf16[1,512,1024]{2,1,0:T(8,128)(2,1)S(1)}, bf16[1,512,1024]{2,1,0:T(8,128)(2,1)}, u32[]{:S(2)}) copy-start(bf16[1,512,1024]{2,1,0:T(8,128)(2,1)} %get-tuple-element.87) | copy-start | bytes 3145732
  280.5 27.1 %copy-start.25 = (bf16[1,512,1024]{2,1,0:T(8,128)(2,1)S(1)}, bf16[1,512,1024]{2,1,0:T(8,128)(2,1)}, u32[]{:S(2)}) copy-start(bf16[1,512,1024]{2,1,0:T(8,128)(2,1)} %get-tuple-element.88) | copy-start | bytes 3145732
  313.6 22.3 %collective-permute-start.15 = (bf16[1,512,1024]{2,1,0:T(8,128)(2,1)S(1)}, bf16[1,512,1024]{2,1,0:T(8,128)(2,1)S(1)}, u32[]{:S(2)}, u32[]{:S(2)}) collective-permute-start(bf16[1,512,1024]{2,1,0:T(8,128)(2,1)S(1)} %fusion.121), channel_id=1, source_target_pairs={{0,1},{1,0},{2,3},{3,2},{4,5},{5,4},{6,7},{7,6},{8,9},{9,8},{10,11... | collective-permute-start | bytes 3145736 | tf_op jit(solution)/shard_map/ppermute | solution.py:188
  315.5 5.6 %collective-permute-start.29 = (bf16[2,2,2,64,768]{4,3,2,0,1:T(8,128)(2,1)S(1)}, bf16[2,2,2,64,768]{4,3,2,0,1:T(8,128)(2,1)S(1)}, u32[]{:S(2)}, u32[]{:S(2)}) collective-permute-start(bf16[2,2,2,64,768]{4,3,2,0,1:T(8,128)(2,1)S(1)} %select_bitcast_fusion), channel_id=1, source_target_pairs={{0,2},{2,0},{4,6},{6,4},{8,10},{10,8},{12,14},{14,12},{16,18},{18,... | collective-permute-start | bytes 2359304 | tf_op jit(solution)/shard_map/ppermute | solution.py:142
  318.6 2.2 collective-permute-start.33
  319.4 3.8 collective-permute-start.25
  321.0 14.8 %collective-permute-start.34 = (bf16[2,2,64,512]{3,2,0,1:T(8,128)(2,1)S(1)}, bf16[2,2,64,512]{3,2,0,1:T(8,128)(2,1)S(1)}, u32[]{:S(2)}, u32[]{:S(2)}) collective-permute-start(bf16[2,2,64,512]{3,2,0,1:T(8,128)(2,1)S(1)} %select_bitcast_fusion.4), channel_id=1, source_target_pairs={{0,4},{2,6},{4,0},{6,2},{8,12},{10,14},{12,8},{14,10},{16,20},{18,... | collective-permute-start | bytes 786440 | tf_op jit(solution)/shard_map/ppermute | solution.py:142
  321.5 14.5 %copy-start.29 = (f32[1,1,1024]{2,1,0:T(1,128)S(1)}, f32[1,1,1024]{2,1,0:T(1,128)}, u32[]{:S(2)}) copy-start(f32[1,1,1024]{2,1,0:T(1,128)} %copy-done.28) | copy-start | bytes 12292
  321.5 45.1 %collective-permute-start.30 = (bf16[2,2,64,768]{3,2,1,0:T(8,128)(2,1)S(1)}, bf16[2,2,64,768]{3,2,1,0:T(8,128)(2,1)S(1)}, u32[]{:S(2)}, u32[]{:S(2)}) collective-permute-start(bf16[2,2,64,768]{3,2,1,0:T(8,128)(2,1)S(1)} %select_bitcast_fusion.3), channel_id=1, source_target_pairs={{0,8},{2,10},{4,12},{6,14},{8,0},{10,2},{12,4},{14,6},{16,24},{18,... | collective-permute-start | bytes 1179656 | tf_op jit(solution)/shard_map/ppermute | solution.py:142
  323.6 12.3 %copy-start.12 = (bf16[2,2,2,64,768]{4,3,2,0,1:T(8,128)(2,1)}, bf16[2,2,2,64,768]{4,3,2,0,1:T(8,128)(2,1)S(1)}, u32[]{:S(2)}) copy-start(bf16[2,2,2,64,768]{4,3,2,0,1:T(8,128)(2,1)S(1)} %fusion.81) | copy-start | bytes 2359300
  323.7 62.3 %collective-permute-start.26 = (bf16[2,2,64,768]{3,2,0,1:T(8,128)(2,1)S(1)}, bf16[2,2,64,768]{3,2,0,1:T(8,128)(2,1)S(1)}, u32[]{:S(2)}, u32[]{:S(2)}) collective-permute-start(bf16[2,2,64,768]{3,2,0,1:T(8,128)(2,1)S(1)} %fusion.145), channel_id=1, source_target_pairs={{0,4},{2,6},{4,0},{6,2},{8,12},{10,14},{12,8},{14,10},{16,20},{18,... | collective-permute-start | bytes 1179656 | tf_op jit(solution)/shard_map/ppermute | solution.py:142
  343.6 3.9 collective-permute-start.16
  343.8 5.0 %collective-permute-start.35 = (bf16[2,64,512]{2,1,0:T(8,128)(2,1)S(1)}, bf16[2,64,512]{2,1,0:T(8,128)(2,1)S(1)}, u32[]{:S(2)}, u32[]{:S(2)}) collective-permute-start(bf16[2,64,512]{2,1,0:T(8,128)(2,1)S(1)} %select_bitcast_fusion.7), channel_id=1, source_target_pairs={{0,8},{2,10},{4,12},{6,14},{8,0},{10,2},{12,4},{14,6},{16,24},{18,... | collective-permute-start | bytes 393224 | tf_op jit(solution)/shard_map/ppermute | solution.py:142
  347.6 1.3 collective-permute-start.17
  349.0 4.3 %collective-permute-start.18 = (bf16[2,6144]{1,0:T(2,128)(2,1)S(1)}, bf16[2,6144]{1,0:T(2,128)(2,1)S(1)}, u32[]{:S(2)}, u32[]{:S(2)}) collective-permute-start(bf16[2,6144]{1,0:T(2,128)(2,1)S(1)} %pad_maximum_fusion.9), channel_id=1, source_target_pairs={{0,4},{2,6},{4,0},{6,2},{8,12},{10,14},{12,8},{14,10},{16,20},{18,... | collective-permute-start | bytes 73736 | tf_op jit(solution)/shard_map/ppermute | solution.py:142
  349.5 9.3 %collective-permute-start.36 = (bf16[64,512]{1,0:T(8,128)(2,1)S(1)}, bf16[64,512]{1,0:T(8,128)(2,1)S(1)}, u32[]{:S(2)}, u32[]{:S(2)}) collective-permute-start(bf16[64,512]{1,0:T(8,128)(2,1)S(1)} %select_bitcast_fusion.10), channel_id=1, source_target_pairs={{0,16},{2,18},{4,20},{6,22},{8,24},{10,26},{12,28},{14,30},{16,0},... | collective-permute-start | bytes 196616 | tf_op jit(solution)/shard_map/ppermute | solution.py:142
  353.5 12.9 %collective-permute-start.19 = (bf16[4,6144]{1,0:T(4,128)(2,1)S(1)}, bf16[4,6144]{1,0:T(4,128)(2,1)S(1)}, u32[]{:S(2)}, u32[]{:S(2)}) collective-permute-start(bf16[4,6144]{1,0:T(4,128)(2,1)S(1)} %pad_maximum_fusion.7), channel_id=1, source_target_pairs={{0,8},{2,10},{4,12},{6,14},{8,0},{10,2},{12,4},{14,6},{16,24},{18,... | collective-permute-start | bytes 147464 | tf_op jit(solution)/shard_map/ppermute | solution.py:142
  366.4 19.6 %copy-start.13 = (bf16[2,2,2,64,768]{4,3,2,0,1:T(8,128)(2,1)S(1)}, bf16[2,2,2,64,768]{4,3,2,0,1:T(8,128)(2,1)}, u32[]{:S(2)}) copy-start(bf16[2,2,2,64,768]{4,3,2,0,1:T(8,128)(2,1)} %copy-done.12) | copy-start | bytes 2359300
  366.5 9.2 %collective-permute-start.20 = (bf16[8,6144]{1,0:T(8,128)(2,1)S(1)}, bf16[8,6144]{1,0:T(8,128)(2,1)S(1)}, u32[]{:S(2)}, u32[]{:S(2)}) collective-permute-start(bf16[8,6144]{1,0:T(8,128)(2,1)S(1)} %pad_maximum_fusion.6), channel_id=1, source_target_pairs={{0,16},{2,18},{4,20},{6,22},{8,24},{10,26},{12,28},{14,30},{16,0},... | collective-permute-start | bytes 294920 | tf_op jit(solution)/shard_map/ppermute | solution.py:142
  375.8 20.9 %copy-start.31 = (bf16[1,1024]{1,0:T(2,128)(2,1)S(1)}, bf16[1,1024]{1,0:T(2,128)(2,1)}, u32[]{:S(2)}) copy-start(bf16[1,1024]{1,0:T(2,128)(2,1)} %param.10) | copy-start | bytes 6148
  375.8 20.9 %copy-start.32 = (f32[1,1024]{1,0:T(1,128)S(1)}, f32[1,1024]{1,0:T(1,128)}, u32[]{:S(2)}) copy-start(f32[1,1024]{1,0:T(1,128)} %get-tuple-element.55) | copy-start | bytes 12292
  376.4 9.4 %collective-permute-start.21 = (f32[8,1024]{1,0:T(8,128)S(1)}, f32[8,1024]{1,0:T(8,128)S(1)}, u32[]{:S(2)}, u32[]{:S(2)}) collective-permute-start(f32[8,1024]{1,0:T(8,128)S(1)} %slice_select_fusion.2), channel_id=1, source_target_pairs={{0,16},{2,18},{4,20},{6,22},{8,24},{10,26},{12,28},{14,30},{16,0},... | collective-permute-start | bytes 98312 | tf_op jit(solution)/shard_map/ppermute | solution.py:142
  376.5 20.7 %collective-permute-start.31 = (bf16[2,64,768]{2,1,0:T(8,128)(2,1)S(1)}, bf16[2,64,768]{2,1,0:T(8,128)(2,1)S(1)}, u32[]{:S(2)}, u32[]{:S(2)}) collective-permute-start(bf16[2,64,768]{2,1,0:T(8,128)(2,1)S(1)} %select_bitcast_fusion.5), channel_id=1, source_target_pairs={{0,16},{2,18},{4,20},{6,22},{8,24},{10,26},{12,28},{14,30},{16,0},... | collective-permute-start | bytes 589832 | tf_op jit(solution)/shard_map/ppermute | solution.py:142
  385.9 4.0 collective-permute-start.22
  390.0 3.7 collective-permute-start.23
  391.5 7.4 %collective-permute-start.27 = (bf16[2,64,768]{2,1,0:T(8,128)(2,1)S(1)}, bf16[2,64,768]{2,1,0:T(8,128)(2,1)S(1)}, u32[]{:S(2)}, u32[]{:S(2)}) collective-permute-start(bf16[2,64,768]{2,1,0:T(8,128)(2,1)S(1)} %select_bitcast_fusion.6), channel_id=1, source_target_pairs={{0,8},{2,10},{4,12},{6,14},{8,0},{10,2},{12,4},{14,6},{16,24},{18,... | collective-permute-start | bytes 589832 | tf_op jit(solution)/shard_map/ppermute | solution.py:142
  393.7 3.0 collective-permute-start.24
  397.4 5.3 %collective-permute-start.32 = (bf16[64,768]{1,0:T(8,128)(2,1)S(1)}, bf16[64,768]{1,0:T(8,128)(2,1)S(1)}, u32[]{:S(2)}, u32[]{:S(2)}) collective-permute-start(bf16[64,768]{1,0:T(8,128)(2,1)S(1)} %select_bitcast_fusion.8), channel_id=1, source_target_pairs={{0,4},{2,6},{4,0},{6,2},{8,12},{10,14},{12,8},{14,10},{16,20},{18,... | collective-permute-start | bytes 294920 | tf_op jit(solution)/shard_map/ppermute | solution.py:142
  399.0 7.4 %collective-permute-start.28 = (bf16[64,768]{1,0:T(8,128)(2,1)S(1)}, bf16[64,768]{1,0:T(8,128)(2,1)S(1)}, u32[]{:S(2)}, u32[]{:S(2)}) collective-permute-start(bf16[64,768]{1,0:T(8,128)(2,1)S(1)} %select_bitcast_fusion.9), channel_id=1, source_target_pairs={{0,16},{2,18},{4,20},{6,22},{8,24},{10,26},{12,28},{14,30},{16,0},... | collective-permute-start | bytes 294920 | tf_op jit(solution)/shard_map/ppermute | solution.py:142
  (15 other events, 33.7 us)
Sparse Core Ops, SparseCore 0:
  10.8 59.0 all-gather.2
  72.6 74.3 all-gather.4
  256.9 118.5 reduce-scatter.1
